TPU v7x, 128 devices: a whole 4x4x4 slice. The times are simulated.
128 devices in a mesh: dp: 32 (over z, y, x_hi), wide: 2 (over x_lo), narrow: 2 (over core).
Axes of the slice: x: 4 (x_hi: 2, x_lo: 2; x = x_hi * 2 + x_lo), y: 4, z: 4, core: 2. Of those that a mesh axis runs over, the one named last changes fastest.
Arguments:
- hidden_in: bfloat16 [32768, 1024], P('dp', 'narrow'), may hold values from -6 to 6
- segment_ids: int32 [32768], P('dp'), may hold values from 0 to 63, never falling along the last dimension, each value on 1 to 2000 neighbouring positions
- qkv_weight: bfloat16 [1024, 16, 3, 64], P('narrow', 'wide'), may hold values from -0.1875 to 0.1875
- qv_bias: float32 [16, 2, 64], P('wide'), may hold values from -3 to 3
- out_weight: bfloat16 [16, 64, 1024], P('wide', None, 'narrow'), may hold values from -1 to 1
- out_bias: float32 [1024], P('narrow'), may hold values from -2 to 2
- norm1_gain: float32 [1024], P('narrow'), may hold values from 0.25 to 1.75
- norm1_shift: float32 [1024], P('narrow'), may hold values from -2 to 2
- up_weight: bfloat16 [1024, 4096], P('narrow', 'wide'), may hold values from -0.1875 to 0.1875
- up_bias: float32 [4096], P('wide'), may hold values from -3 to 3
- down_weight: bfloat16 [4096, 1024], P('wide', 'narrow'), may hold values from -0.1875 to 0.1875
- down_bias: float32 [1024], P('narrow'), may hold values from -2 to 2
- norm2_gain: float32 [1024], P('narrow'), may hold values from 0.25 to 1.75
- norm2_shift: float32 [1024], P('narrow'), may hold values from -2 to 2
- out_grad: bfloat16 [32768, 1024], P(('dp', 'wide'), 'narrow'), may hold values from -6 to 6
Outputs:
- hidden_out: bfloat16 [32768, 1024], P(('dp', 'wide'), 'narrow')
- input_grad: float32 [32768, 1024], P(('dp', 'wide'), 'narrow')
- qkv_weight_grad: float32 [1024, 16, 3, 64], P('narrow', 'wide')
- qv_bias_grad: float32 [16, 2, 64], P('wide')
- out_weight_grad: float32 [16, 64, 1024], P('wide', None, 'narrow')
- out_bias_grad: float32 [1024], P('narrow')
- norm1_gain_grad: float32 [1024], P('narrow')
- norm1_shift_grad: float32 [1024], P('narrow')
- up_weight_grad: float32 [1024, 4096], P('narrow', 'wide')
- up_bias_grad: float32 [4096], P('wide')
- down_weight_grad: float32 [4096, 1024], P('wide', 'narrow')
- down_bias_grad: float32 [1024], P('narrow')
- norm2_gain_grad: float32 [1024], P('narrow')
- norm2_shift_grad: float32 [1024], P('narrow')
All inputs are finite; a program needn't handle non-finite values.
Results may differ from a plain program's by a relative error of at most 0.03.
Values may be sent and summed in bfloat16 or wider, within the bound.
A program may use at most 128 MiB of HBM per device.

v0:
```python
from functools import partial

import jax
import jax.numpy as jnp
from jax import lax
from jax.sharding import PartitionSpec as P

D = 1024
SEQ_LEN = 512


EPSILON = 1e-05
NEGATIVE = -1000000000.0


def for_sending(shard):
    return jax.tree.map(lambda a: a.astype(jnp.bfloat16) if a.dtype == jnp.float32 else a, shard)


def contract(left_side, right_side, left_dim, right_dim):
    return lax.dot_general(
        left_side,
        right_side,
        (((left_dim,), (right_dim,)), ((), ())),
        preferred_element_type=jnp.float32,
    )


def narrow_rows_sum(terms):
    return lax.psum_scatter(terms, "narrow", scatter_dimension=0, tiled=True)


def narrow_rows_gather(pieces):
    return lax.all_gather(for_sending(pieces), "narrow", axis=0, tiled=True).astype(pieces.dtype)


def wide_rows_gather(pieces):
    return lax.all_gather(pieces, "wide", axis=0, tiled=True)


def wide_rows_sum(left_side, right_side, right_dim, row_count):
    block = lax.slice_in_dim(left_side, 0, row_count * lax.axis_size("wide"), axis=0)
    return lax.psum_scatter(
        contract(block, right_side, 1, right_dim).astype(jnp.bfloat16),
        "wide",
        scatter_dimension=0,
        tiled=True,
    ).astype(jnp.float32)


def narrow_stats(first, second):
    return lax.psum((first, second), "narrow")


def norm_forward(rows_in, norm_gain, norm_shift):
    sums, squares = narrow_stats(jnp.sum(rows_in, -1), jnp.sum(rows_in * rows_in, -1))
    center = sums / D
    inverse = lax.rsqrt(squares / D - center * center + EPSILON)
    normed = (rows_in - center[:, None]) * inverse[:, None]
    return (normed * norm_gain + norm_shift, normed, inverse)


def norm_backward(grad_rows, normed, inverse, norm_gain):
    scaled = grad_rows * norm_gain
    first, second = narrow_stats(jnp.sum(scaled, -1), jnp.sum(scaled * normed, -1))
    return inverse[:, None] * (scaled - first[:, None] / D - normed * (second[:, None] / D))


def gain_parts(grad_rows, normed):
    return (jnp.sum(grad_rows * normed, 0), jnp.sum(grad_rows, 0))


def by_sequence(tensor, seq_len):
    return tensor.reshape((tensor.shape[0] // seq_len, seq_len) + tensor.shape[1:])


def masked_scores(tile_probe_vectors, block_keys, segment_block, score_scale):
    attention_scores = (
        jnp.einsum(
            "yvx,bvx->vyb", tile_probe_vectors, block_keys, preferred_element_type=jnp.float32
        )
        * score_scale
    )
    same_doc = segment_block[:, None] == segment_block[None, :]
    return jnp.where(same_doc[None], attention_scores, NEGATIVE)


def attend(query_rows, every_key, every_value, segment, seq_len, score_scale):
    row_count, head_count, head_width = query_rows.shape

    def one_sequence(blocks):
        tile_probe_vectors, block_keys, block_values, segment_block = blocks
        attention_scores = masked_scores(tile_probe_vectors, block_keys, segment_block, score_scale)
        row_peak = jnp.max(attention_scores, -1, keepdims=True)
        raised = jnp.exp(attention_scores - row_peak)
        row_total = jnp.sum(raised, -1, keepdims=True)
        attention_weights = (raised / row_total).astype(jnp.bfloat16)
        context_rows = jnp.einsum(
            "njv,vnz->jnz", attention_weights, block_values, preferred_element_type=jnp.float32
        )
        return (context_rows.astype(jnp.bfloat16), (row_peak + jnp.log(row_total))[..., 0])

    context_rows, logarithm_normalizer = lax.map(
        one_sequence,
        (
            by_sequence(query_rows, seq_len),
            by_sequence(every_key, seq_len),
            by_sequence(every_value, seq_len),
            by_sequence(segment, seq_len),
        ),
    )
    return (context_rows.reshape(row_count, head_count * head_width), logarithm_normalizer)


def attend_back(
    query_rows,
    every_key,
    every_value,
    segment,
    logarithm_normalizer,
    grad_context,
    seq_len,
    score_scale,
):
    row_count, head_count, head_width = query_rows.shape

    def one_sequence(blocks):
        tile_probe_vectors, block_keys, block_values, segment_block, total_block, gradient_block = (
            blocks
        )
        attention_scores = masked_scores(tile_probe_vectors, block_keys, segment_block, score_scale)
        probs = jnp.exp(attention_scores - total_block[..., None])
        grad_values = jnp.einsum(
            "dvz,vdq->zdq",
            probs.astype(jnp.bfloat16),
            gradient_block,
            preferred_element_type=jnp.float32,
        )
        grad_probs = jnp.einsum(
            "yvx,bvx->vyb", gradient_block, block_values, preferred_element_type=jnp.float32
        )
        inner = jnp.sum(grad_probs * probs, -1, keepdims=True)
        logit_sensitivity = (probs * (grad_probs - inner)).astype(jnp.bfloat16)
        grad_queries = (
            jnp.einsum(
                "njv,vnz->jnz", logit_sensitivity, block_keys, preferred_element_type=jnp.float32
            )
            * score_scale
        )
        grad_keys = (
            jnp.einsum(
                "dvz,vdq->zdq",
                logit_sensitivity,
                tile_probe_vectors,
                preferred_element_type=jnp.float32,
            )
            * score_scale
        )
        return jnp.stack(
            [
                grad_queries.astype(jnp.bfloat16),
                grad_keys.astype(jnp.bfloat16),
                grad_values.astype(jnp.bfloat16),
            ],
            2,
        )

    stacked = lax.map(
        one_sequence,
        (
            by_sequence(query_rows, seq_len),
            by_sequence(every_key, seq_len),
            by_sequence(every_value, seq_len),
            by_sequence(segment, seq_len),
            logarithm_normalizer,
            by_sequence(grad_context, seq_len),
        ),
    )
    return stacked.reshape(row_count, head_count * 3 * head_width)


def split_qkv(projected, qv_bias, row_count, heads_here, head_width):
    qkv_four = projected.reshape(row_count, heads_here, 3, head_width)
    query_rows = (qkv_four[:, :, 0] + qv_bias[:, 0]).astype(jnp.bfloat16)
    every_key = qkv_four[:, :, 1].astype(jnp.bfloat16)
    every_value = (qkv_four[:, :, 2] + qv_bias[:, 1]).astype(jnp.bfloat16)
    return (query_rows, every_key, every_value)


def bias_pair(grad_qkv, heads_here, head_width):
    qkv_sums = jnp.sum(grad_qkv, 0, dtype=jnp.float32).reshape(heads_here, 3, head_width)
    return jnp.stack([qkv_sums[:, 0], qkv_sums[:, 2]], 1)


def per_device(
    hidden_in,
    segment_ids,
    qkv_weight,
    qv_bias,
    out_weight,
    out_bias,
    norm1_gain,
    norm1_shift,
    up_weight,
    up_bias,
    down_weight,
    down_bias,
    norm2_gain,
    norm2_shift,
    out_grad,
):
    token_count, half_width = hidden_in.shape
    heads_here = qkv_weight.shape[1]
    head_width = qkv_weight.shape[3]
    wide_rows = out_grad.shape[0]
    narrow_count = lax.axis_size("narrow")
    narrow_at = lax.axis_index("narrow")
    wide_start = lax.axis_index("wide") * wide_rows
    score_scale = head_width ** (-0.5)
    qkv_flat = qkv_weight.reshape(half_width, heads_here * 3 * head_width)
    out_flat = out_weight.reshape(heads_here * head_width, half_width)
    gelu_exact = partial(jax.nn.gelu, approximate=False)
    att_rows = token_count // narrow_count
    qkv_part = narrow_rows_sum(jnp.dot(hidden_in, qkv_flat, preferred_element_type=jnp.float32))
    att_segment = lax.dynamic_slice_in_dim(segment_ids, narrow_at * att_rows, att_rows)
    query_rows, every_key, every_value = split_qkv(
        qkv_part, qv_bias, att_rows, heads_here, head_width
    )
    context_rows, logarithm_normalizer = attend(
        query_rows, every_key, every_value, att_segment, SEQ_LEN, score_scale
    )
    context_full = narrow_rows_gather(context_rows)
    hidden_mine = lax.dynamic_slice_in_dim(hidden_in, wide_start, wide_rows, 0).astype(jnp.float32)
    attn_mine = wide_rows_sum(context_full, out_flat, 0, wide_rows) + out_bias
    norm1_mine, normed1, inverse1 = norm_forward(hidden_mine + attn_mine, norm1_gain, norm1_shift)
    mixed_full = wide_rows_gather(norm1_mine.astype(jnp.bfloat16))
    upward = (
        narrow_rows_sum(jnp.dot(mixed_full, up_weight, preferred_element_type=jnp.float32))
        + up_bias
    )
    activated_full = narrow_rows_gather(gelu_exact(upward).astype(jnp.bfloat16))
    downward = wide_rows_sum(activated_full, down_weight, 0, wide_rows) + down_bias
    out_rows, normed2, inverse2 = norm_forward(norm1_mine + downward, norm2_gain, norm2_shift)
    hidden_out = out_rows.astype(jnp.bfloat16)
    cotangent = out_grad.astype(jnp.float32)
    grad_res2 = norm_backward(cotangent, normed2, inverse2, norm2_gain)
    gain2_part, shift2_part = gain_parts(cotangent, normed2)
    grad_down_full = wide_rows_gather(grad_res2.astype(jnp.bfloat16))
    grad_hidden = narrow_rows_sum(contract(grad_down_full, down_weight, 1, 1))
    gelu_value, gelu_pull = jax.vjp(gelu_exact, upward)
    expansion_cotangent_entire = narrow_rows_gather(gelu_pull(grad_hidden)[0].astype(jnp.bfloat16))
    down_weight_grad = contract(activated_full, grad_down_full, 0, 0)
    down_bias_grad = jnp.sum(grad_down_full, 0, dtype=jnp.float32)
    up_weight_grad = contract(mixed_full, expansion_cotangent_entire, 0, 0)
    up_bias_grad = jnp.sum(expansion_cotangent_entire, 0, dtype=jnp.float32)
    grad_mixed = grad_res2 + wide_rows_sum(expansion_cotangent_entire, up_weight, 1, wide_rows)
    grad_res1 = norm_backward(grad_mixed, normed1, inverse1, norm1_gain)
    gain1_part, shift1_part = gain_parts(grad_mixed, normed1)
    grad_attn_full = wide_rows_gather(grad_res1.astype(jnp.bfloat16))
    out_weight_grad = contract(context_full, grad_attn_full, 0, 0).reshape(
        heads_here, head_width, half_width
    )
    out_bias_grad = jnp.sum(grad_attn_full, 0, dtype=jnp.float32)
    grad_context = narrow_rows_sum(contract(grad_attn_full, out_flat, 1, 1))
    grad_context = grad_context.astype(jnp.bfloat16).reshape(att_rows, heads_here, head_width)
    grad_qkv = attend_back(
        query_rows,
        every_key,
        every_value,
        att_segment,
        logarithm_normalizer,
        grad_context,
        SEQ_LEN,
        score_scale,
    )
    grad_qkv_full = narrow_rows_gather(grad_qkv)
    qkv_weight_grad = contract(hidden_in, grad_qkv_full, 0, 0).reshape(
        half_width, heads_here, 3, head_width
    )
    qv_bias_grad = bias_pair(grad_qkv_full, heads_here, head_width)
    input_grad = grad_res1 + wide_rows_sum(grad_qkv_full, qkv_flat, 1, wide_rows)
    summed = (
        lax.psum(qkv_weight_grad.astype(jnp.bfloat16), "dp").astype(jnp.float32),
        lax.psum(qv_bias_grad.astype(jnp.bfloat16), "dp").astype(jnp.float32),
        lax.psum(out_weight_grad.astype(jnp.bfloat16), "dp").astype(jnp.float32),
        lax.psum(out_bias_grad.astype(jnp.bfloat16), "dp").astype(jnp.float32),
        lax.psum(up_weight_grad.astype(jnp.bfloat16), "dp").astype(jnp.float32),
        lax.psum(up_bias_grad.astype(jnp.bfloat16), "dp").astype(jnp.float32),
        lax.psum(down_weight_grad.astype(jnp.bfloat16), "dp").astype(jnp.float32),
        lax.psum(down_bias_grad.astype(jnp.bfloat16), "dp").astype(jnp.float32),
    )
    norm_sums = lax.psum((gain1_part, shift1_part, gain2_part, shift2_part), ("dp", "wide"))
    return (
        hidden_out,
        input_grad,
        summed[0],
        summed[1],
        summed[2],
        summed[3],
        norm_sums[0],
        norm_sums[1],
        summed[4],
        summed[5],
        summed[6],
        summed[7],
        norm_sums[2],
        norm_sums[3],
    )


def solution(mesh):
    return jax.shard_map(
        per_device,
        mesh=mesh,
        in_specs=(
            P("dp", "narrow"),
            P("dp"),
            P("narrow", "wide", None, None),
            P("wide", None, None),
            P("wide", None, "narrow"),
            P("narrow"),
            P("narrow"),
            P("narrow"),
            P("narrow", "wide"),
            P("wide"),
            P("wide", "narrow"),
            P("narrow"),
            P("narrow"),
            P("narrow"),
            P(("dp", "wide"), "narrow"),
        ),
        out_specs=(
            P(("dp", "wide"), "narrow"),
            P(("dp", "wide"), "narrow"),
            P("narrow", "wide", None, None),
            P("wide", None, None),
            P("wide", None, "narrow"),
            P("narrow"),
            P("narrow"),
            P("narrow"),
            P("narrow", "wide"),
            P("wide"),
            P("wide", "narrow"),
            P("narrow"),
            P("narrow"),
            P("narrow"),
        ),
        check_vma=False,
    )
```

profile of v0, /device:TPU:0, one launch (start us, length us, event | category | flops | bytes accessed | tf_op | source)
XLA Modules:
  0.0 861.9 jit_solution(1268937737068449119)
XLA Ops:
  7.2 6.3 fusion.53
  13.7 0.6 copy-done.25
  14.6 18.8 %reduce-scatter.9.cloned.1.call-done = f32[512,1536]{1,0:T(8,128)} async-done(((f32[1024,1536]{1,0:T(8,128)}), f32[512,1536]{1,0:T(8,128)}) %reduce-scatter.9.cloned.1.call-update) | async-done | bytes 3145744 | tf_op jit(solution)/shard_map/reduce_scatter | solution.py:30
  33.3 3.5 copy.38
  36.9 3.1 fusion.52
  40.0 1.2 fusion
  41.2 2.0 copy-done.2
  43.2 3.7 fusion.15
  46.9 13.2 %all-gather.8.cloned.1.call-done = bf16[1024,512]{0,1:T(8,128)(2,1)} async-done(((bf16[512,512]{0,1:T(8,128)(2,1)}), bf16[1024,512]{0,1:T(8,128)(2,1)}) %all-gather.8.cloned.1.call-update) | async-done | bytes 1048592 | tf_op jit(solution)/shard_map/all_gather | solution.py:34
  60.2 3.1 convolution_convert_fusion.4
  63.3 24.3 %reduce-scatter.11.cloned.1.call-done = bf16[512,512]{1,0:T(8,128)(2,1)} async-done(((bf16[1024,512]{1,0:T(8,128)(2,1)}), bf16[512,512]{1,0:T(8,128)(2,1)}) %reduce-scatter.11.cloned.1.call-update) | async-done | bytes 524304 | tf_op jit(solution)/shard_map/reduce_scatter | solution.py:43
  87.6 1.4 fusion.35
  89.0 2.5 all-reduce.4
  91.5 2.1 fusion.34
  93.7 24.9 %all-gather.10.cloned.1.call-done = bf16[1024,512]{1,0:T(8,128)(2,1)} async-done(((bf16[512,512]{1,0:T(8,128)(2,1)}), bf16[1024,512]{1,0:T(8,128)(2,1)}) %all-gather.10.cloned.1.call-update) | async-done | bytes 1048592 | tf_op jit(solution)/shard_map/all_gather | solution.py:38
  118.6 7.5 fusion.54
  126.3 20.5 %reduce-scatter.13.cloned.1.call-done = f32[512,2048]{1,0:T(8,128)} async-done(((f32[1024,2048]{1,0:T(8,128)}), f32[512,2048]{1,0:T(8,128)}) %reduce-scatter.13.cloned.1.call-update) | async-done | bytes 4194320 | tf_op jit(solution)/shard_map/reduce_scatter | solution.py:30
  146.8 11.6 %multiply_convert_fusion.1 = (bf16[512,2048]{1,0:T(8,128)(2,1)}, f32[512,2048]{1,0:T(8,128)}) fusion(f32[512,2048]{1,0:T(8,128)} %reduce-scatter.13.cloned.1.call-done, f32[2048]{0:T(1024)S(1)} %copy-done.19), kind=kLoop, calls=%fused_computation.13 | loop fusion | flops 69206016 | bytes 10493952 | tf_op jit(solution)/shard_map/convert_element_type | solution.py:241
  158.5 17.8 %all-gather.12.cloned.1.call-done = bf16[1024,2048]{1,0:T(8,128)(2,1)} async-done(((bf16[512,2048]{1,0:T(8,128)(2,1)}), bf16[1024,2048]{1,0:T(8,128)(2,1)}) %all-gather.12.cloned.1.call-update) | async-done | bytes 4194320 | tf_op jit(solution)/shard_map/all_gather | solution.py:34
  176.3 5.5 convolution_convert_fusion.6
  181.8 24.3 %reduce-scatter.15.cloned.1.call-done = bf16[512,512]{1,0:T(8,128)(2,1)} async-done(((bf16[1024,512]{1,0:T(8,128)(2,1)}), bf16[512,512]{1,0:T(8,128)(2,1)}) %reduce-scatter.15.cloned.1.call-update) | async-done | bytes 524304 | tf_op jit(solution)/shard_map/reduce_scatter | solution.py:43
  206.2 2.6 fusion.45
  208.8 2.4 all-reduce.3
  211.2 1.8 fusion.29
  213.0 2.5 all-reduce.2
  215.5 3.0 fusion.47
  218.5 24.9 %all-gather.14.cloned.1.call-done = bf16[1024,512]{1,0:T(8,128)(2,1)} async-done(((bf16[512,512]{1,0:T(8,128)(2,1)}), bf16[1024,512]{1,0:T(8,128)(2,1)}) %all-gather.14.cloned.1.call-update) | async-done | bytes 1048592 | tf_op jit(solution)/shard_map/all_gather | solution.py:38
  243.4 6.8 fusion.55
  250.3 20.6 %reduce-scatter.17.cloned.1.call-done = f32[512,2048]{1,0:T(8,128)} async-done(((f32[1024,2048]{1,0:T(8,128)}), f32[512,2048]{1,0:T(8,128)}) %reduce-scatter.17.cloned.1.call-update) | async-done | bytes 4194320 | tf_op jit(solution)/shard_map/reduce_scatter | solution.py:30
  270.9 6.6 add_convert_fusion
  277.6 17.8 %all-gather.16.cloned.1.call-done = bf16[1024,2048]{1,0:T(8,128)(2,1)} async-done(((bf16[512,2048]{1,0:T(8,128)(2,1)}), bf16[1024,2048]{1,0:T(8,128)(2,1)}) %all-gather.16.cloned.1.call-update) | async-done | bytes 4194320 | tf_op jit(solution)/shard_map/all_gather | solution.py:34
  295.4 6.2 convolution_convert_fusion.5
  301.7 24.3 %reduce-scatter.19.cloned.1.call-done = bf16[512,512]{1,0:T(8,128)(2,1)} async-done(((bf16[1024,512]{1,0:T(8,128)(2,1)}), bf16[512,512]{1,0:T(8,128)(2,1)}) %reduce-scatter.19.cloned.1.call-update) | async-done | bytes 524304 | tf_op jit(solution)/shard_map/reduce_scatter | solution.py:43
  326.0 1.7 multiply_reduce_fusion.1
  327.6 2.7 all-reduce.1
  330.3 2.7 fusion.46
  333.1 24.9 %all-gather.18.cloned.1.call-done = bf16[1024,512]{1,0:T(8,128)(2,1)} async-done(((bf16[512,512]{1,0:T(8,128)(2,1)}), bf16[1024,512]{1,0:T(8,128)(2,1)}) %all-gather.18.cloned.1.call-update) | async-done | bytes 1048592 | tf_op jit(solution)/shard_map/all_gather | solution.py:38
  358.0 3.3 fusion.56
  361.3 13.3 %reduce-scatter.21.cloned.1.call-done = f32[512,512]{1,0:T(8,128)} async-done(((f32[1024,512]{1,0:T(8,128)}), f32[512,512]{1,0:T(8,128)}) %reduce-scatter.21.cloned.1.call-update) | async-done | bytes 1048592 | tf_op jit(solution)/shard_map/reduce_scatter | solution.py:30
  374.6 1.3 convert_element_type.176
  376.1 4.9 fusion.23
  381.1 4.7 multiply_reduce_fusion
  385.9 2.5 multiply_convert_fusion
  388.4 1.4 fusion.21
  389.8 0.8 fusion.22
  390.9 1.2 copy.45
  392.2 16.3 %all-gather.20.cloned.1.call-done = bf16[1024,1536]{0,1:T(8,128)(2,1)} async-done(((bf16[512,1536]{0,1:T(8,128)(2,1)}), bf16[1024,1536]{0,1:T(8,128)(2,1)}) %all-gather.20.cloned.1.call-update) | async-done | bytes 3145744 | tf_op jit(solution)/shard_map/all_gather | solution.py:34
  408.5 5.1 convolution_convert_fusion.3
  414.0 6.0 convolution_convert_fusion
  420.1 3.8 convolution_convert_fusion.1
  423.9 1.5 convolution_convert_fusion.7
  425.4 3.0 convolution_convert_fusion.2
  428.6 3.0 reduce_sum.187
  431.6 190.5 %all-reduce = (f32[512]{0:T(512)}, f32[512]{0:T(512)}, f32[512]{0:T(512)}, f32[512]{0:T(512)}) all-reduce(f32[512]{0:T(512)S(1)} %get-tuple-element.51, f32[512]{0:T(512)S(1)} %get-tuple-element.66, f32[512]{0:T(512)S(1)} %get-tuple-element.61, f32[512]{0:T(512)S(1)} %get-tuple-element.70), channel_id=1, replica_groups=mesh['dp'=32,'wide'=2,'narrow'=2] {'dp','wide'}, use_global_device_ids=true, to_apply=%region_34.35 | all-reduce | flops 2048 | bytes 16384 | tf_op jit(solution)/shard_map/psum | solution.py:292
  622.4 2.4 reduce.3
  624.9 177.3 %all-reduce.5 = (bf16[8,2,64]{2,1,0:T(2,128)(2,1)S(1)}, bf16[512]{0:T(512)(128)(2,1)S(1)}, bf16[2048]{0:T(1024)(128)(2,1)S(1)}, bf16[512]{0:T(512)(128)(2,1)S(1)}) all-reduce(bf16[8,2,64]{2,1,0:T(2,128)(2,1)S(1)} %pad_maximum_fusion.1, bf16[512]{0:T(512)(128)(2,1)S(1)} %reduce_sum.184, ...), channel_id=1, replica_groups=mesh['dp'=32,'wide'=2,'narrow'=2] {'dp'}, use_global_device_ids=true, to_apply=%region_29.30 | all-reduce | flops 4096 | bytes 16384 | tf_op jit(solution)/shard_map/psum | solution.py:284
  803.3 0.6 convert_element_type.192
  803.9 0.6 convert_element_type.199
  804.5 2.2 convert_add_fusion
  806.7 37.2 %all-reduce.9.cloned.1.call-done = (bf16[512,8,3,64]{0,3,2,1:T(8,128)(2,1)}, bf16[8,64,512]{2,1,0:T(8,128)(2,1)}, bf16[512,2048]{1,0:T(8,128)(2,1)}, bf16[2048,512]{1,0:T(8,128)(2,1)}) async-done(((bf16[512,8,3,64]{0,3,2,1:T(8,128)(2,1)}, bf16[8,64,512]{2,1,0:T(8,128)(2,1)}, bf16[512,2048]{1,0:T(8,128)(2,1)}, bf16[2048,512]{1,0:T(8,128)(2,1)}), (bf16[512,8,3,64]{0,3,2,1:T(8,128)(2,1)}, ...) | async-done | bytes 6291472 | tf_op jit(solution)/shard_map/psum | solution.py:283
  843.9 2.3 convert_element_type.195
  846.2 3.5 convert_element_type.190
  849.7 2.7 convert_element_type.198
  852.3 2.6 convert_element_type.201
  (110 shorter events, 4.0 us)
Async XLA Ops:
  7.2 169.1 %copy-start = (bf16[2048,512]{1,0:T(8,128)(2,1)S(1)}, bf16[2048,512]{1,0:T(8,128)(2,1)}, u32[]{:S(2)}) copy-start(bf16[2048,512]{1,0:T(8,128)(2,1)} %param.25) | copy-start | bytes 6291460
  7.2 26.1 %reduce-scatter.9.cloned.1.call-start = ((), (), s32[]{:S(2)}) async-start(), calls=%async_computation.8 | async-start | bytes 9437184 | tf_op jit(solution)/shard_map/reduce_scatter | solution.py:30
  13.6 0.7 copy-start.25
  13.6 0.8 copy-start.21
  13.6 46.6 %all-gather.8.cloned.1.call-start = ((), (), s32[]{:S(2)}) async-start(), calls=%async_computation.9 | async-start | bytes 1572864 | tf_op jit(solution)/shard_map/all_gather | solution.py:34
  40.0 3.2 copy-start.2
  46.9 40.8 %copy-start.6 = (bf16[1024,512]{1,0:T(8,128)(2,1)S(1)}, bf16[1024,512]{1,0:T(8,128)(2,1)}, u32[]{:S(2)}) copy-start(bf16[1024,512]{1,0:T(8,128)(2,1)} %param.15) | copy-start | bytes 3145732
  46.9 40.8 %copy-start.17 = (f32[512]{0:T(512)S(1)}, f32[512]{0:T(512)}, u32[]{:S(2)}) copy-start(f32[512]{0:T(512)} %param.20) | copy-start | bytes 6148
  46.9 44.6 %copy-start.18 = (f32[512]{0:T(512)S(1)}, f32[512]{0:T(512)}, u32[]{:S(2)}) copy-start(f32[512]{0:T(512)} %param.21) | copy-start | bytes 6148
  46.9 44.6 %copy-start.22 = (f32[512]{0:T(512)S(1)}, f32[512]{0:T(512)}, u32[]{:S(2)}) copy-start(f32[512]{0:T(512)} %param.22) | copy-start | bytes 6148
  46.9 40.7 %reduce-scatter.11.cloned.1.call-start = ((), (), s32[]{:S(2)}) async-start(), calls=%async_computation.10 | async-start | bytes 1572864 | tf_op jit(solution)/shard_map/reduce_scatter | solution.py:43
  63.3 55.3 %all-gather.10.cloned.1.call-start = ((), (), s32[]{:S(2)}) async-start(), calls=%async_computation.11 | async-start | bytes 1572864 | tf_op jit(solution)/shard_map/all_gather | solution.py:38
  93.7 53.1 %reduce-scatter.13.cloned.1.call-start = ((), (), s32[]{:S(2)}) async-start(), calls=%async_computation.12 | async-start | bytes 12582912 | tf_op jit(solution)/shard_map/reduce_scatter | solution.py:30
  126.1 20.7 %copy-start.19 = (f32[2048]{0:T(1024)S(1)}, f32[2048]{0:T(1024)}, u32[]{:S(2)}) copy-start(f32[2048]{0:T(1024)} %param.24) | copy-start | bytes 24580
  126.1 50.2 %all-gather.12.cloned.1.call-start = ((), (), s32[]{:S(2)}) async-start(), calls=%async_computation.13 | async-start | bytes 6291456 | tf_op jit(solution)/shard_map/all_gather | solution.py:34
  158.4 47.8 %copy-start.4 = (bf16[512,512]{1,0:T(8,128)(2,1)S(1)}, bf16[512,512]{1,0:T(8,128)(2,1)}, u32[]{:S(2)}) copy-start(bf16[512,512]{1,0:T(8,128)(2,1)} %reduce-scatter.11.cloned.1.call-done) | copy-start | bytes 1572868
  158.4 47.8 %copy-start.24 = (f32[512]{0:T(512)S(1)}, f32[512]{0:T(512)}, u32[]{:S(2)}) copy-start(f32[512]{0:T(512)} %param.26) | copy-start | bytes 6148
  158.4 52.8 %copy-start.14 = (bf16[512,512]{1,0:T(8,128)(2,1)S(1)}, bf16[512,512]{1,0:T(8,128)(2,1)}, u32[]{:S(2)}) copy-start(bf16[512,512]{1,0:T(8,128)(2,1)} %param.29) | copy-start | bytes 1572868
  158.4 52.8 %copy-start.20 = (f32[512]{0:T(512)S(1)}, f32[512]{0:T(512)}, u32[]{:S(2)}) copy-start(f32[512]{0:T(512)} %param.27) | copy-start | bytes 6148
  158.4 47.7 %reduce-scatter.15.cloned.1.call-start = ((), (), s32[]{:S(2)}) async-start(), calls=%async_computation.14 | async-start | bytes 1572864 | tf_op jit(solution)/shard_map/reduce_scatter | solution.py:43
  181.8 33.7 %copy-start.23 = (f32[512]{0:T(512)S(1)}, f32[512]{0:T(512)}, u32[]{:S(2)}) copy-start(f32[512]{0:T(512)} %param.28) | copy-start | bytes 6148
  181.8 61.6 %all-gather.14.cloned.1.call-start = ((), (), s32[]{:S(2)}) async-start(), calls=%async_computation.15 | async-start | bytes 1572864 | tf_op jit(solution)/shard_map/all_gather | solution.py:38
  218.5 52.5 %reduce-scatter.17.cloned.1.call-start = ((), (), s32[]{:S(2)}) async-start(), calls=%async_computation.16 | async-start | bytes 12582912 | tf_op jit(solution)/shard_map/reduce_scatter | solution.py:30
  250.2 45.2 %all-gather.16.cloned.1.call-start = ((), (), s32[]{:S(2)}) async-start(), calls=%async_computation.17 | async-start | bytes 6291456 | tf_op jit(solution)/shard_map/all_gather | solution.py:34
  277.5 48.5 %copy-start.5 = (f32[512,512]{1,0:T(8,128)S(1)}, f32[512,512]{1,0:T(8,128)}, u32[]{:S(2)}) copy-start(f32[512,512]{1,0:T(8,128)} %get-tuple-element.94) | copy-start | bytes 3145732
  277.5 48.4 %copy-start.7 = (bf16[1024,512]{1,0:T(8,128)(2,1)S(1)}, bf16[1024,512]{1,0:T(8,128)(2,1)}, u32[]{:S(2)}) copy-start(bf16[1024,512]{1,0:T(8,128)(2,1)} %param.15) | copy-start | bytes 3145732
  277.5 48.4 %reduce-scatter.19.cloned.1.call-start = ((), (), s32[]{:S(2)}) async-start(), calls=%async_computation.18 | async-start | bytes 1572864 | tf_op jit(solution)/shard_map/reduce_scatter | solution.py:43
  301.6 56.4 %copy-start.16 = (bf16[8,64,512]{2,1,0:T(8,128)(2,1)S(1)}, bf16[8,64,512]{2,1,0:T(8,128)(2,1)}, u32[]{:S(2)}) copy-start(bf16[8,64,512]{2,1,0:T(8,128)(2,1)} %param.19) | copy-start | bytes 1572868
  301.6 56.3 %all-gather.18.cloned.1.call-start = ((), (), s32[]{:S(2)}) async-start(), calls=%async_computation.19 | async-start | bytes 1572864 | tf_op jit(solution)/shard_map/all_gather | solution.py:38
  333.0 41.6 %reduce-scatter.21.cloned.1.call-start = ((), (), s32[]{:S(2)}) async-start(), calls=%async_computation.20 | async-start | bytes 3145728 | tf_op jit(solution)/shard_map/reduce_scatter | solution.py:30
  361.3 47.3 %all-gather.20.cloned.1.call-start = ((), (), s32[]{:S(2)}) async-start(), calls=%async_computation.21 | async-start | bytes 4718592 | tf_op jit(solution)/shard_map/all_gather | solution.py:34
  376.1 5.0 copy-start.3
  376.1 9.7 %slice-start = ((s8[8388608]{0:T(1024)(128)(4,1)}), s8[4194304]{0:T(1024)(128)(4,1)S(1)}, s32[]{:S(2)}) async-start(s8[8388608]{0:T(1024)(128)(4,1)} %bitcast.80), calls=%async_computation.24 | async-start | bytes 8388608
  381.1 4.8 slice-start.1
  392.1 21.9 %copy-start.15 = (bf16[1024,512]{1,0:T(8,128)(2,1)S(1)}, bf16[1024,512]{1,0:T(8,128)(2,1)}, u32[]{:S(2)}) copy-start(bf16[1024,512]{1,0:T(8,128)(2,1)} %all-gather.14.cloned.1.call-done) | copy-start | bytes 3145732
  392.1 412.4 %reduce-scatter.23.cloned.1.call-start = ((), (), s32[]{:S(2)}) async-start(), calls=%async_computation.22 | async-start | bytes 1572864 | tf_op jit(solution)/shard_map/reduce_scatter | solution.py:43
  413.7 430.2 %all-reduce.9.cloned.1.call-start = ((), (), s32[]{:S(2)}) async-start(), calls=%async_computation.23 | async-start | bytes 12582912 | tf_op jit(solution)/shard_map/psum | solution.py:283
  414.0 6.1 copy-start.8
  414.0 6.1 copy-start.27
  420.1 3.8 copy-start.10
  420.1 3.8 copy-start.26
  420.1 5.3 copy-start.11
  428.6 375.9 %copy-start.9 = (f32[512,512]{1,0:T(8,128)S(1)}, f32[512,512]{1,0:T(8,128)}, u32[]{:S(2)}) copy-start(f32[512,512]{1,0:T(8,128)} %get-tuple-element.92) | copy-start | bytes 3145732
  843.9 5.8 copy-start.13
  849.7 2.7 copy-start.12
  849.7 5.3 copy-start.1
Sparse Core Ops, SparseCore 0:
  13.7 19.5 reduce-scatter.8
  47.0 13.1 all-gather.7
  63.4 24.1 reduce-scatter.10
  93.8 24.7 all-gather.9
  126.2 20.5 reduce-scatter.12
  158.5 17.7 all-gather.11
  181.9 24.1 reduce-scatter.14
  218.6 24.7 all-gather.13
  250.4 20.5 reduce-scatter.16
  277.6 17.7 all-gather.15
  301.7 24.1 reduce-scatter.18
  333.1 24.7 all-gather.17
  361.4 13.1 reduce-scatter.20
  392.3 16.2 all-gather.19
  413.8 24.2 reduce-scatter.22
  441.9 401.9 all-reduce.8
where the time goes:
time: 870 us; the launch traced here: 862 us
  blocking collectives  378 us (43%)
  waiting for transfers between devices  323 us (37%)
  matrix products  76.7 us (9%)
  other arithmetic  60.2 us (7%)
  between operations  14.7 us (2%)
    psum x1, blocking collectives, per_device(): lax.psum((gain1_part, shift1_part, gain2_part, shift2_part), ('dp', 'wide'))  191 us
    psum x1, blocking collectives, per_device(): lax.psum(qv_bias_grad.astype(jnp.bfloat16), 'dp').astype(jnp.float32)  177 us
    all_gather x3, waiting for transfers between devices, wide_rows_gather(): return lax.all_gather(pieces, 'wide', axis=0, tiled=True)  74.7 us
    reduce_scatter x4, waiting for transfers between devices, narrow_rows_sum(): return lax.psum_scatter(terms, 'narrow', scatter_dimension=0, tiled=True)  73.1 us
    reduce_scatter x4, waiting for transfers between devices, wide_rows_sum(): lax.psum_scatter(contract(block, right_side, 1, right_dim).astype(jnp.bfl...  72.9 us
    all_gather x4, waiting for transfers between devices, narrow_rows_gather(): lax.all_gather(for_sending(pieces), 'narrow', axis=0, tiled=True)  65.2 us
    dot_general x10, matrix products, contract(): lax.dot_general(left_side, right_side, (((left_dim,), (right_dim,)), ((),...  44.3 us
    psum x1, waiting for transfers between devices, per_device(): lax.psum(qkv_weight_grad.astype(jnp.bfloat16), 'dp').astype(jnp.float32)  37.2 us
  transfers between devices with their start and end apart: 16, of which 15 were waited for; matrix products, arithmetic and copies ran while one was open for 3% of the time, Pallas kernels for 0%

commit v1 on v0

--- a/solution.py
+++ b/solution.py
@@ -3,6 +3,8 @@
 import jax
 import jax.numpy as jnp
 from jax import lax
+from jax.experimental import pallas as pl
+from jax.experimental.pallas import tpu as pltpu
 from jax.sharding import PartitionSpec as P
 
 D = 1024
@@ -190,6 +192,212 @@
 def bias_pair(grad_qkv, heads_here, head_width):
     qkv_sums = jnp.sum(grad_qkv, 0, dtype=jnp.float32).reshape(heads_here, 3, head_width)
     return jnp.stack([qkv_sums[:, 0], qkv_sums[:, 2]], 1)
+
+
+MESH = pl.DeviceIdType.MESH
+BF = jnp.bfloat16
+F32 = jnp.float32
+PACK = 512
+
+
+def partner_table():
+    dp = lax.axis_index("dp")
+    z, y, xh = dp // 8, (dp // 2) % 4, dp % 2
+    wide, narrow = lax.axis_index("wide"), lax.axis_index("narrow")
+
+    def at(z, y, xh):
+        return (z * 8 + y * 2 + xh, wide, narrow)
+
+    def parity(v):
+        return (v % 2 + v // 2) % 2
+
+    return {
+        "y1": (at(z, y + 1 - 2 * (y % 2), xh), parity(y)),
+        "z1": (at(z + 1 - 2 * (z % 2), y, xh), parity(z)),
+        "y3": (at(z, 3 - y, xh), y // 2),
+        "z3": (at(3 - z, y, xh), z // 2),
+        "xh": (at(z, y, 1 - xh), xh),
+        "wide": ((dp, 1 - wide, narrow), wide),
+    }
+
+
+ORDERS = (
+    ("y1", "z1", "y3", "z3"),
+    ("z1", "y3", "z3", "y1"),
+    ("y3", "z3", "y1", "z1"),
+    ("z3", "y1", "z1", "y3"),
+)
+SMALL_ORDER = ("wide", "y1", "z1", "y3", "z3", "xh")
+
+
+class Summing:
+    def __init__(self, buf, recv, out, send_sem, recv_sem, base, rows, recv_base, table):
+        self.buf, self.recv, self.out = buf, recv, out
+        self.send_sem, self.recv_sem, self.table = send_sem, recv_sem, table
+        self.quarter = rows // 4
+        self.offsets, self.places = [], []
+        place = recv_base
+        for q, order in enumerate(ORDERS):
+            offset, size = base + q * self.quarter, self.quarter
+            trail, slots = [offset], []
+            for name in order:
+                size = size // 2
+                offset = pl.multiple_of(offset + table[name][1] * size, 16)
+                trail.append(offset)
+                slots.append(place)
+                place += size
+            slots.append(place)
+            place += size
+            self.offsets.append(trail)
+            self.places.append(slots)
+        self.sent = []
+
+    def size(self, level):
+        return self.quarter >> level
+
+    def copy(self, q, step, src, dst, name):
+        return pltpu.make_async_remote_copy(
+            src_ref=src,
+            dst_ref=dst,
+            send_sem=self.send_sem.at[q, step],
+            recv_sem=self.recv_sem.at[q, step],
+            device_id=self.table[name][0],
+            device_id_type=MESH,
+        )
+
+    def make(self, q, step):
+        if step < 4:
+            name, size = ORDERS[q][step], self.size(step + 1)
+            start = self.offsets[q][step] + (1 - self.table[name][1]) * size
+            src = self.buf.at[pl.ds(pl.multiple_of(start, 16), size), :]
+            dst = self.recv.at[pl.ds(self.places[q][step], size), :]
+        elif step == 4:
+            name, size = "xh", self.size(4)
+            src = self.buf.at[pl.ds(self.offsets[q][4], size), :]
+            dst = self.recv.at[pl.ds(self.places[q][4], size), :]
+        else:
+            level = 9 - step
+            name, size = ORDERS[q][level - 1], self.size(level)
+            src = self.out.at[pl.ds(self.offsets[q][level], size), :]
+            dst = src
+        return self.copy(q, step, src, dst, name)
+
+    def begin(self, q, step):
+        copy = self.make(q, step)
+        copy.start()
+        self.sent.append(copy)
+
+    def take(self, q, step):
+        self.make(q, step).wait_recv()
+        if step <= 4:
+            level = min(step + 1, 4)
+            size = self.size(level)
+            target = self.out if step == 4 else self.buf
+            chunk = 32
+            offset, place = self.offsets[q][level], self.places[q][step]
+
+            def add(i, carry):
+                here = pl.ds(pl.multiple_of(offset + i * chunk, 16), chunk)
+                there = pl.ds(pl.multiple_of(place + i * chunk, 16), chunk)
+                total = self.buf[here, :].astype(F32) + self.recv[there, :].astype(F32)
+                target[here, :] = total.astype(BF)
+                return carry
+
+            lax.fori_loop(0, size // chunk, add, 0)
+
+    def open(self):
+        for q in range(4):
+            self.begin(q, 0)
+
+    def advance(self, step):
+        for q in range(4):
+            self.take(q, step)
+            if step < 8:
+                self.begin(q, step + 1)
+
+    def close(self):
+        for copy in self.sent:
+            copy.wait_send()
+
+
+def sum_kernel(buf_in, small_in, out, small_out, buf, recv, small_recv, ss, rs, small_ss, small_rs):
+    table = partner_table()
+    barrier = pltpu.get_barrier_semaphore()
+    for device, _ in table.values():
+        pl.semaphore_signal(barrier, inc=1, device_id=device, device_id_type=MESH)
+    pl.semaphore_wait(barrier, len(table))
+    rows = buf_in.shape[0]
+    work = Summing(buf_in, recv, out, ss, rs, 0, rows, 0, table)
+    work.buf = buf
+    chunk = 64
+
+    def stage(i, carry):
+        here = pl.ds(pl.multiple_of(i * chunk, 16), chunk)
+        buf[here, :] = buf_in[here, :]
+        return carry
+
+    lax.fori_loop(0, rows // chunk, stage, 0)
+    work.open()
+    small_sent = []
+    held = small_in[...]
+    for step in range(9):
+        if step < len(SMALL_ORDER):
+            small_out[step] = held
+            first = 8 if step == 0 else 0
+            copy = pltpu.make_async_remote_copy(
+                src_ref=small_out.at[step, pl.ds(first, 16 - first)],
+                dst_ref=small_recv.at[step, pl.ds(first, 16 - first)],
+                send_sem=small_ss.at[step],
+                recv_sem=small_rs.at[step],
+                device_id=table[SMALL_ORDER[step]][0],
+                device_id_type=MESH,
+            )
+            copy.start()
+            small_sent.append(copy)
+        work.advance(step)
+        if step < len(SMALL_ORDER):
+            copy.wait_recv()
+            if step == 0:
+                top = held[:8]
+                held = jnp.concatenate([top, held[8:] + small_recv[0, 8:, :]], 0)
+            else:
+                held = held + small_recv[step]
+    small_out[len(SMALL_ORDER)] = held
+    work.close()
+    for copy in small_sent:
+        copy.wait_send()
+
+
+def sum_over_dp(packed, small):
+    rows = packed.shape[0]
+    steps = len(SMALL_ORDER)
+    vmem = pl.BlockSpec(memory_space=pltpu.VMEM)
+    out, small_out = pl.pallas_call(
+        sum_kernel,
+        out_shape=(
+            jax.ShapeDtypeStruct((rows, PACK), BF),
+            jax.ShapeDtypeStruct((steps + 1, 16, PACK), F32),
+        ),
+        in_specs=[vmem, vmem],
+        out_specs=(vmem, vmem),
+        scratch_shapes=[
+            pltpu.VMEM((rows, PACK), BF),
+            pltpu.VMEM((rows, PACK), BF),
+            pltpu.VMEM((steps, 16, PACK), F32),
+            pltpu.SemaphoreType.DMA((4, 9)),
+            pltpu.SemaphoreType.DMA((4, 9)),
+            pltpu.SemaphoreType.DMA((steps,)),
+            pltpu.SemaphoreType.DMA((steps,)),
+        ],
+        compiler_params=pltpu.CompilerParams(
+            collective_id=1, has_side_effects=True, vmem_limit_bytes=56 * 2**20
+        ),
+    )(packed, small)
+    return out, small_out[steps]
+
+
+def pack_columns(matrix):
+    return [matrix[:, i : i + PACK] for i in range(0, matrix.shape[1], PACK)]
 
 
 def per_device(
@@ -279,17 +487,46 @@
     )
     qv_bias_grad = bias_pair(grad_qkv_full, heads_here, head_width)
     input_grad = grad_res1 + wide_rows_sum(grad_qkv_full, qkv_flat, 1, wide_rows)
+    packed = jnp.concatenate(
+        [
+            piece.astype(BF)
+            for piece in pack_columns(qkv_weight_grad.reshape(half_width, -1))
+            + [out_weight_grad.reshape(-1, half_width)]
+            + pack_columns(up_weight_grad)
+            + [down_weight_grad]
+        ],
+        0,
+    )
+    small = jnp.concatenate(
+        [
+            qv_bias_grad.reshape(-1, PACK),
+            out_bias_grad[None],
+            down_bias_grad[None],
+            up_bias_grad.reshape(-1, PACK),
+            jnp.stack([gain1_part, shift1_part, gain2_part, shift2_part]),
+            jnp.zeros((4, PACK), F32),
+        ],
+        0,
+    )
+    total, small = sum_over_dp(packed, small)
+    total = total.astype(F32)
+    heads_rows = heads_here * head_width
+    qkv_rows = 3 * heads_rows
+    up_start = qkv_rows + heads_rows
+    up_rows = up_weight.shape[1] // PACK * half_width
+    blocks = lambda rows: jnp.concatenate(jnp.split(rows, rows.shape[0] // half_width, 0), 1)
+    qv_bias_sum = small[0:2].reshape(heads_here, 2, head_width)
     summed = (
-        lax.psum(qkv_weight_grad.astype(jnp.bfloat16), "dp").astype(jnp.float32),
-        lax.psum(qv_bias_grad.astype(jnp.bfloat16), "dp").astype(jnp.float32),
-        lax.psum(out_weight_grad.astype(jnp.bfloat16), "dp").astype(jnp.float32),
-        lax.psum(out_bias_grad.astype(jnp.bfloat16), "dp").astype(jnp.float32),
-        lax.psum(up_weight_grad.astype(jnp.bfloat16), "dp").astype(jnp.float32),
-        lax.psum(up_bias_grad.astype(jnp.bfloat16), "dp").astype(jnp.float32),
-        lax.psum(down_weight_grad.astype(jnp.bfloat16), "dp").astype(jnp.float32),
-        lax.psum(down_bias_grad.astype(jnp.bfloat16), "dp").astype(jnp.float32),
-    )
-    norm_sums = lax.psum((gain1_part, shift1_part, gain2_part, shift2_part), ("dp", "wide"))
+        blocks(total[:qkv_rows]).reshape(half_width, heads_here, 3, head_width),
+        qv_bias_sum,
+        total[qkv_rows:up_start].reshape(heads_here, head_width, half_width),
+        small[2],
+        blocks(total[up_start : up_start + up_rows]),
+        small[4:8].reshape(-1),
+        total[up_start + up_rows :],
+        small[3],
+    )
+    norm_sums = (small[8], small[9], small[10], small[11])
     return (
         hidden_out,
         input_grad,

time: 870 us -> 573 us (0.66)
  blocking collectives: 378 us -> 21.3 us
  Pallas kernels: 0 us -> 93.5 us
  waiting for transfers between devices: 323 us -> 276 us
  local copies, waits for them, and re-layouts: 8.01 us -> 30.2 us
    psum x2 -> x0, blocking collectives: 368 us -> none  [the longest x1 191 us: per_device(): lax.psum((gain1_part, shift1_part, gain2_part, shift2_part), ('dp', 'wide'))]
    pallas_call x0 -> x1, Pallas kernels: none -> 93.5 us  [sum_over_dp(): pl.pallas_call(sum_kernel, out_shape=(jax.ShapeDtypeStruct((rows, PACK),...]
    psum x1 -> x0, waiting for transfers between devices: 37.2 us -> none  [per_device(): lax.psum(qkv_weight_grad.astype(jnp.bfloat16), 'dp').astype(jnp.float32)]
    convert_element_type x8 -> x0, other arithmetic: 13.4 us -> none  [the longest x1 3.5 us: per_device(): lax.psum(qkv_weight_grad.astype(jnp.bfloat16), 'dp').astype(jnp.float32)]
    psum x4, blocking collectives: 10.1 us -> 21.3 us  [narrow_stats(): return lax.psum((first, second), 'narrow')]
    all_gather x4, waiting for transfers between devices: 65.2 us -> 55.6 us  [narrow_rows_gather(): lax.all_gather(for_sending(pieces), 'narrow', axis=0, tiled=True)]
  transfers between devices with their start and end apart: 16 -> 15, of which waited for: 15 -> 14; matrix products, arithmetic and copies ran while one was open for 3% -> 9% of each run, Pallas kernels for 0% -> 16%
where the time goes in v1:
time: 573 us; the launch traced here: 570 us
  waiting for transfers between devices  276 us (48%)
  Pallas kernels  93.5 us (16%)
  matrix products  79.9 us (14%)
  other arithmetic  53.2 us (9%)
  local copies, waits for them, and re-layouts  30.2 us (5%)
  blocking collectives  21.3 us (4%)
  between operations  14.5 us (3%)
    pallas_call x1, Pallas kernels, sum_over_dp(): pl.pallas_call(sum_kernel, out_shape=(jax.ShapeDtypeStruct((rows, PACK),...  93.5 us
    all_gather x3, waiting for transfers between devices, wide_rows_gather(): return lax.all_gather(pieces, 'wide', axis=0, tiled=True)  74.7 us
    reduce_scatter x4, waiting for transfers between devices, narrow_rows_sum(): return lax.psum_scatter(terms, 'narrow', scatter_dimension=0, tiled=True)  73 us
    reduce_scatter x4, waiting for transfers between devices, wide_rows_sum(): lax.psum_scatter(contract(block, right_side, 1, right_dim).astype(jnp.bfl...  72.9 us
    all_gather x4, waiting for transfers between devices, narrow_rows_gather(): lax.all_gather(for_sending(pieces), 'narrow', axis=0, tiled=True)  55.6 us
    dot_general x10, matrix products, contract(): lax.dot_general(left_side, right_side, (((left_dim,), (right_dim,)), ((),...  47.5 us
    psum x4, blocking collectives, narrow_stats(): return lax.psum((first, second), 'narrow')  21.3 us
    convert_element_type x1, other arithmetic, per_device(): activated_full = narrow_rows_gather(gelu_exact(upward).astype(jnp.bfloat16))  11.6 us
  transfers between devices with their start and end apart: 15, of which 14 were waited for; matrix products, arithmetic and copies ran while one was open for 9% of the time, Pallas kernels for 16%

profile of v1, /device:TPU:0, one launch (start us, length us, event | category | flops | bytes accessed | tf_op | source)
XLA Modules:
  0.0 569.9 jit_solution(780968367273378618)
XLA Ops:
  7.2 6.3 %fusion.58 = f32[1024,1536]{1,0:T(8,128)} fusion(bf16[1024,512]{1,0:T(8,128)(2,1)} %param.15, bf16[512,1536]{0,1:T(8,128)(2,1)} %bitcast.127), kind=kOutput, calls=%fused_computation.118 | convolution fusion | flops 1610612736 | bytes 8912896 | tf_op jit(solution)/shard_map/dot_general | solution.py:432
  14.6 18.8 %reduce-scatter.9.cloned.1.call-done = f32[512,1536]{1,0:T(8,128)} async-done(((f32[1024,1536]{1,0:T(8,128)}), f32[512,1536]{1,0:T(8,128)}) %reduce-scatter.9.cloned.1.call-update) | async-done | bytes 3145744 | tf_op jit(solution)/shard_map/reduce_scatter | solution.py:32
  33.3 3.5 copy.39
  36.9 3.1 fusion.57
  40.0 1.2 fusion
  41.2 2.1 copy-done.2
  43.2 3.7 fusion.17
  47.0 13.2 %all-gather.8.cloned.1.call-done = bf16[1024,512]{0,1:T(8,128)(2,1)} async-done(((bf16[512,512]{0,1:T(8,128)(2,1)}), bf16[1024,512]{0,1:T(8,128)(2,1)}) %all-gather.8.cloned.1.call-update) | async-done | bytes 1048592 | tf_op jit(solution)/shard_map/all_gather | solution.py:36
  60.2 3.1 convolution_convert_fusion.4
  63.4 24.3 %reduce-scatter.11.cloned.1.call-done = bf16[512,512]{1,0:T(8,128)(2,1)} async-done(((bf16[1024,512]{1,0:T(8,128)(2,1)}), bf16[512,512]{1,0:T(8,128)(2,1)}) %reduce-scatter.11.cloned.1.call-update) | async-done | bytes 524304 | tf_op jit(solution)/shard_map/reduce_scatter | solution.py:45
  87.7 1.4 fusion.38
  89.1 2.5 all-reduce.3
  91.5 2.1 fusion.37
  93.8 24.9 %all-gather.10.cloned.1.call-done = bf16[1024,512]{1,0:T(8,128)(2,1)} async-done(((bf16[512,512]{1,0:T(8,128)(2,1)}), bf16[1024,512]{1,0:T(8,128)(2,1)}) %all-gather.10.cloned.1.call-update) | async-done | bytes 1048592 | tf_op jit(solution)/shard_map/all_gather | solution.py:40
  118.6 7.5 %fusion.59 = f32[1024,2048]{1,0:T(8,128)} fusion(bf16[1024,512]{1,0:T(8,128)(2,1)} %all-gather.10.cloned.1.call-done, bf16[512,2048]{1,0:T(8,128)(2,1)} %param.23), kind=kOutput, calls=%fused_computation.119 | convolution fusion | flops 2147483648 | bytes 11534336 | tf_op jit(solution)/shard_map/dot_general | solution.py:446
  126.5 20.4 %reduce-scatter.13.cloned.1.call-done = f32[512,2048]{1,0:T(8,128)} async-done(((f32[1024,2048]{1,0:T(8,128)}), f32[512,2048]{1,0:T(8,128)}) %reduce-scatter.13.cloned.1.call-update) | async-done | bytes 4194320 | tf_op jit(solution)/shard_map/reduce_scatter | solution.py:32
  146.8 11.6 %multiply_convert_fusion.1 = (bf16[512,2048]{1,0:T(8,128)(2,1)}, f32[512,2048]{1,0:T(8,128)}) fusion(f32[512,2048]{1,0:T(8,128)} %reduce-scatter.13.cloned.1.call-done, f32[2048]{0:T(1024)S(1)} %copy-done.17), kind=kLoop, calls=%fused_computation.16 | loop fusion | flops 69206016 | bytes 10493952 | tf_op jit(solution)/shard_map/convert_element_type | solution.py:449
  158.5 17.8 %all-gather.12.cloned.1.call-done = bf16[1024,2048]{1,0:T(8,128)(2,1)} async-done(((bf16[512,2048]{1,0:T(8,128)(2,1)}), bf16[1024,2048]{1,0:T(8,128)(2,1)}) %all-gather.12.cloned.1.call-update) | async-done | bytes 4194320 | tf_op jit(solution)/shard_map/all_gather | solution.py:36
  176.3 5.5 convolution_convert_fusion.6
  181.9 24.3 %reduce-scatter.15.cloned.1.call-done = bf16[512,512]{1,0:T(8,128)(2,1)} async-done(((bf16[1024,512]{1,0:T(8,128)(2,1)}), bf16[512,512]{1,0:T(8,128)(2,1)}) %reduce-scatter.15.cloned.1.call-update) | async-done | bytes 524304 | tf_op jit(solution)/shard_map/reduce_scatter | solution.py:45
  206.2 2.6 fusion.48
  208.8 2.4 all-reduce.2
  211.3 1.8 fusion.32
  213.0 2.5 all-reduce.1
  215.5 3.0 fusion.50
  218.5 24.9 %all-gather.14.cloned.1.call-done = bf16[1024,512]{1,0:T(8,128)(2,1)} async-done(((bf16[512,512]{1,0:T(8,128)(2,1)}), bf16[1024,512]{1,0:T(8,128)(2,1)}) %all-gather.14.cloned.1.call-update) | async-done | bytes 1048592 | tf_op jit(solution)/shard_map/all_gather | solution.py:40
  243.4 6.8 %fusion.60 = f32[1024,2048]{1,0:T(8,128)} fusion(bf16[1024,512]{1,0:T(8,128)(2,1)} %all-gather.14.cloned.1.call-done, bf16[2048,512]{1,0:T(8,128)(2,1)S(1)} %copy-done), kind=kOutput, calls=%fused_computation.120 | convolution fusion | flops 2147483648 | bytes 11534336 | tf_op jit(solution)/shard_map/dot_general | solution.py:23
  250.3 20.6 %reduce-scatter.17.cloned.1.call-done = f32[512,2048]{1,0:T(8,128)} async-done(((f32[1024,2048]{1,0:T(8,128)}), f32[512,2048]{1,0:T(8,128)}) %reduce-scatter.17.cloned.1.call-update) | async-done | bytes 4194320 | tf_op jit(solution)/shard_map/reduce_scatter | solution.py:32
  271.0 6.6 %add_convert_fusion = bf16[512,2048]{1,0:T(8,128)(2,1)} fusion(f32[512,2048]{1,0:T(8,128)} %reduce-scatter.17.cloned.1.call-done, f32[512,2048]{1,0:T(8,128)} %get-tuple-element.103, f32[512,2048]{1,0:T(8,128)} %reduce-scatter.13.cloned.1.call-done, f32[2048]{0:T(1024)S(1)} %copy-done.17), kind=kLoop, calls=%fused_computation.15 | loop fusion | flops 15728640 | bytes 14688256 | tf_op jit(solution)/shard_map/convert_element_type | solution.py:459
  277.6 17.8 %all-gather.16.cloned.1.call-done = bf16[1024,2048]{1,0:T(8,128)(2,1)} async-done(((bf16[512,2048]{1,0:T(8,128)(2,1)}), bf16[1024,2048]{1,0:T(8,128)(2,1)}) %all-gather.16.cloned.1.call-update) | async-done | bytes 4194320 | tf_op jit(solution)/shard_map/all_gather | solution.py:36
  295.4 6.2 %convolution_convert_fusion.5 = bf16[1024,512]{1,0:T(8,128)(2,1)} fusion(bf16[1024,2048]{1,0:T(8,128)(2,1)} %all-gather.16.cloned.1.call-done, bf16[512,2048]{1,0:T(8,128)(2,1)} %param.23), kind=kOutput, calls=%fused_computation.45 | convolution fusion | flops 2148007936 | bytes 7340032 | tf_op jit(solution)/shard_map/dot_general | solution.py:23
  301.7 24.3 %reduce-scatter.19.cloned.1.call-done = bf16[512,512]{1,0:T(8,128)(2,1)} async-done(((bf16[1024,512]{1,0:T(8,128)(2,1)}), bf16[512,512]{1,0:T(8,128)(2,1)}) %reduce-scatter.19.cloned.1.call-update) | async-done | bytes 524304 | tf_op jit(solution)/shard_map/reduce_scatter | solution.py:45
  326.0 1.7 multiply_reduce_fusion.1
  327.7 14.0 %all-reduce = (f32[512]{0:T(512)S(1)}, f32[512]{0:T(512)S(1)}) all-reduce(f32[512]{0:T(512)S(1)} %get-tuple-element.78, f32[512]{0:T(512)S(1)} %get-tuple-element.81), channel_id=1, replica_groups=mesh['dp'=32,'wide'=2,'narrow'=2] {'narrow'}, use_global_device_ids=true, to_apply=%region_23.24 | all-reduce | flops 1024 | bytes 8192 | tf_op jit(solution)/shard_map/psum | solution.py:54
  341.6 2.7 fusion.49
  344.4 24.9 %all-gather.18.cloned.1.call-done = bf16[1024,512]{1,0:T(8,128)(2,1)} async-done(((bf16[512,512]{1,0:T(8,128)(2,1)}), bf16[1024,512]{1,0:T(8,128)(2,1)}) %all-gather.18.cloned.1.call-update) | async-done | bytes 1048592 | tf_op jit(solution)/shard_map/all_gather | solution.py:40
  369.3 3.3 fusion.61
  372.6 13.3 %reduce-scatter.21.cloned.1.call-done = f32[512,512]{1,0:T(8,128)} async-done(((f32[1024,512]{1,0:T(8,128)}), f32[512,512]{1,0:T(8,128)}) %reduce-scatter.21.cloned.1.call-update) | async-done | bytes 1048592 | tf_op jit(solution)/shard_map/reduce_scatter | solution.py:32
  385.9 1.3 convert_element_type.149
  387.4 4.9 fusion.26
  392.4 4.7 multiply_reduce_fusion
  397.2 2.5 multiply_convert_fusion
  399.7 1.4 fusion.24
  401.1 0.8 fusion.25
  402.2 1.2 copy.46
  403.7 2.8 convert_reduce_fusion
  406.6 6.3 %convolution_convert_fusion.1 = bf16[512,2048]{1,0:T(8,128)(2,1)} fusion(bf16[1024,512]{1,0:T(8,128)(2,1)} %all-gather.10.cloned.1.call-done, bf16[1024,2048]{1,0:T(8,128)(2,1)} %all-gather.16.cloned.1.call-done), kind=kOutput, calls=%fused_computation.34 | convolution fusion | flops 2148532224 | bytes 7340032 | tf_op jit(solution)/shard_map/dot_general | solution.py:23
  413.1 6.8 %all-gather.20.cloned.1.call-done = bf16[1024,1536]{0,1:T(8,128)(2,1)} async-done(((bf16[512,1536]{0,1:T(8,128)(2,1)}), bf16[1024,1536]{0,1:T(8,128)(2,1)}) %all-gather.20.cloned.1.call-update) | async-done | bytes 3145744 | tf_op jit(solution)/shard_map/all_gather | solution.py:36
  419.8 2.4 convert_reduce_fusion.1
  422.4 5.2 convolution_convert_fusion.3
  427.6 3.8 fusion.13
  433.9 1.5 fusion.23
  435.5 0.9 slice_dynamic-update-slice_fusion.3
  436.4 0.9 slice_dynamic-update-slice_fusion.2
  438.9 1.3 concatenate.13.small_in
  440.2 5.9 %fusion.12.buf_in = bf16[6144,512]{1,0:T(8,128)(2,1)} fusion(bf16[6144,512]{1,0:T(8,128)(2,1)} %slice_dynamic-update-slice_fusion, bf16[1024,2048]{1,0:T(8,128)(2,1)} %all-gather.12.cloned.1.call-done, bf16[1024,512]{1,0:T(8,128)(2,1)S(1)} %copy-done.13), kind=kOutput, calls=%fused_computation.33 | convolution fusion | flops 2148532224 | bytes 7340032 | tf_op jit(solution)/shard_map/dot_general | solution.py:23
  446.0 93.5 %shard_map.254 = (bf16[6144,512]{1,0:T(8,128)(2,1)}, f32[7,16,512]{2,1,0:T(8,128)}) custom-call(bf16[6144,512]{1,0:T(8,128)(2,1)} %fusion.12.buf_in, f32[16,512]{1,0:T(8,128)} %concatenate.13.small_in), custom_call_target="tpu_custom_call" | custom-call | tf_op jit(solution)/shard_map/pallas_call | solution.py:375
  542.3 4.3 slice.143
  546.6 2.7 fusion.53
  549.3 1.9 pad_maximum_fusion.1
  551.2 3.5 copy.47
  554.7 1.5 fusion.54
  556.2 4.8 pad_maximum_fusion
  561.0 2.2 convert_add_fusion
  (113 shorter events, 10.2 us)
Async XLA Ops:
  7.2 169.2 %copy-start = (bf16[2048,512]{1,0:T(8,128)(2,1)S(1)}, bf16[2048,512]{1,0:T(8,128)(2,1)}, u32[]{:S(2)}) copy-start(bf16[2048,512]{1,0:T(8,128)(2,1)} %param.25) | copy-start | bytes 6291460
  7.2 26.1 %reduce-scatter.9.cloned.1.call-start = ((), (), s32[]{:S(2)}) async-start(), calls=%async_computation.8 | async-start | bytes 9437184 | tf_op jit(solution)/shard_map/reduce_scatter | solution.py:32
  13.6 0.7 copy-start.23
  13.6 0.8 copy-start.19
  13.6 46.6 %all-gather.8.cloned.1.call-start = ((), (), s32[]{:S(2)}) async-start(), calls=%async_computation.9 | async-start | bytes 1572864 | tf_op jit(solution)/shard_map/all_gather | solution.py:36
  40.0 3.3 copy-start.2
  46.9 40.8 %copy-start.7 = (bf16[1024,512]{1,0:T(8,128)(2,1)S(1)}, bf16[1024,512]{1,0:T(8,128)(2,1)}, u32[]{:S(2)}) copy-start(bf16[1024,512]{1,0:T(8,128)(2,1)} %param.15) | copy-start | bytes 3145732
  46.9 40.8 %copy-start.15 = (f32[512]{0:T(512)S(1)}, f32[512]{0:T(512)}, u32[]{:S(2)}) copy-start(f32[512]{0:T(512)} %param.20) | copy-start | bytes 6148
  46.9 44.6 %copy-start.16 = (f32[512]{0:T(512)S(1)}, f32[512]{0:T(512)}, u32[]{:S(2)}) copy-start(f32[512]{0:T(512)} %param.21) | copy-start | bytes 6148
  46.9 44.6 %copy-start.20 = (f32[512]{0:T(512)S(1)}, f32[512]{0:T(512)}, u32[]{:S(2)}) copy-start(f32[512]{0:T(512)} %param.22) | copy-start | bytes 6148
  46.9 40.7 %reduce-scatter.11.cloned.1.call-start = ((), (), s32[]{:S(2)}) async-start(), calls=%async_computation.10 | async-start | bytes 1572864 | tf_op jit(solution)/shard_map/reduce_scatter | solution.py:45
  63.3 55.3 %all-gather.10.cloned.1.call-start = ((), (), s32[]{:S(2)}) async-start(), calls=%async_computation.11 | async-start | bytes 1572864 | tf_op jit(solution)/shard_map/all_gather | solution.py:40
  93.7 53.1 %reduce-scatter.13.cloned.1.call-start = ((), (), s32[]{:S(2)}) async-start(), calls=%async_computation.12 | async-start | bytes 12582912 | tf_op jit(solution)/shard_map/reduce_scatter | solution.py:32
  126.1 20.7 %copy-start.17 = (f32[2048]{0:T(1024)S(1)}, f32[2048]{0:T(1024)}, u32[]{:S(2)}) copy-start(f32[2048]{0:T(1024)} %param.24) | copy-start | bytes 24580
  126.2 50.2 %all-gather.12.cloned.1.call-start = ((), (), s32[]{:S(2)}) async-start(), calls=%async_computation.13 | async-start | bytes 6291456 | tf_op jit(solution)/shard_map/all_gather | solution.py:36
  158.4 47.7 %copy-start.5 = (bf16[512,512]{1,0:T(8,128)(2,1)S(1)}, bf16[512,512]{1,0:T(8,128)(2,1)}, u32[]{:S(2)}) copy-start(bf16[512,512]{1,0:T(8,128)(2,1)} %reduce-scatter.11.cloned.1.call-done) | copy-start | bytes 1572868
  158.5 47.7 %copy-start.22 = (f32[512]{0:T(512)S(1)}, f32[512]{0:T(512)}, u32[]{:S(2)}) copy-start(f32[512]{0:T(512)} %param.26) | copy-start | bytes 6148
  158.5 52.8 %copy-start.12 = (bf16[512,512]{1,0:T(8,128)(2,1)S(1)}, bf16[512,512]{1,0:T(8,128)(2,1)}, u32[]{:S(2)}) copy-start(bf16[512,512]{1,0:T(8,128)(2,1)} %param.29) | copy-start | bytes 1572868
  158.5 52.8 %copy-start.18 = (f32[512]{0:T(512)S(1)}, f32[512]{0:T(512)}, u32[]{:S(2)}) copy-start(f32[512]{0:T(512)} %param.27) | copy-start | bytes 6148
  158.5 47.7 %reduce-scatter.15.cloned.1.call-start = ((), (), s32[]{:S(2)}) async-start(), calls=%async_computation.14 | async-start | bytes 1572864 | tf_op jit(solution)/shard_map/reduce_scatter | solution.py:45
  181.8 33.7 %copy-start.21 = (f32[512]{0:T(512)S(1)}, f32[512]{0:T(512)}, u32[]{:S(2)}) copy-start(f32[512]{0:T(512)} %param.28) | copy-start | bytes 6148
  181.8 61.6 %all-gather.14.cloned.1.call-start = ((), (), s32[]{:S(2)}) async-start(), calls=%async_computation.15 | async-start | bytes 1572864 | tf_op jit(solution)/shard_map/all_gather | solution.py:40
  218.5 52.5 %reduce-scatter.17.cloned.1.call-start = ((), (), s32[]{:S(2)}) async-start(), calls=%async_computation.16 | async-start | bytes 12582912 | tf_op jit(solution)/shard_map/reduce_scatter | solution.py:32
  250.3 45.1 %all-gather.16.cloned.1.call-start = ((), (), s32[]{:S(2)}) async-start(), calls=%async_computation.17 | async-start | bytes 6291456 | tf_op jit(solution)/shard_map/all_gather | solution.py:36
  277.5 48.4 %copy-start.6 = (f32[512,512]{1,0:T(8,128)S(1)}, f32[512,512]{1,0:T(8,128)}, u32[]{:S(2)}) copy-start(f32[512,512]{1,0:T(8,128)} %get-tuple-element.100) | copy-start | bytes 3145732
  277.5 48.4 %copy-start.8 = (bf16[1024,512]{1,0:T(8,128)(2,1)S(1)}, bf16[1024,512]{1,0:T(8,128)(2,1)}, u32[]{:S(2)}) copy-start(bf16[1024,512]{1,0:T(8,128)(2,1)} %param.15) | copy-start | bytes 3145732
  277.6 48.4 %reduce-scatter.19.cloned.1.call-start = ((), (), s32[]{:S(2)}) async-start(), calls=%async_computation.18 | async-start | bytes 1572864 | tf_op jit(solution)/shard_map/reduce_scatter | solution.py:45
  301.6 67.7 %copy-start.14 = (bf16[8,64,512]{2,1,0:T(8,128)(2,1)S(1)}, bf16[8,64,512]{2,1,0:T(8,128)(2,1)}, u32[]{:S(2)}) copy-start(bf16[8,64,512]{2,1,0:T(8,128)(2,1)} %param.19) | copy-start | bytes 1572868
  301.6 67.6 %all-gather.18.cloned.1.call-start = ((), (), s32[]{:S(2)}) async-start(), calls=%async_computation.19 | async-start | bytes 1572864 | tf_op jit(solution)/shard_map/all_gather | solution.py:40
  344.3 41.6 %reduce-scatter.21.cloned.1.call-start = ((), (), s32[]{:S(2)}) async-start(), calls=%async_computation.20 | async-start | bytes 3145728 | tf_op jit(solution)/shard_map/reduce_scatter | solution.py:32
  372.6 47.3 %all-gather.20.cloned.1.call-start = ((), (), s32[]{:S(2)}) async-start(), calls=%async_computation.21 | async-start | bytes 4718592 | tf_op jit(solution)/shard_map/all_gather | solution.py:36
  387.4 5.0 copy-start.4
  387.4 9.7 %slice-start = ((s8[8388608]{0:T(1024)(128)(4,1)}), s8[4194304]{0:T(1024)(128)(4,1)S(1)}, s32[]{:S(2)}) async-start(s8[8388608]{0:T(1024)(128)(4,1)} %bitcast.95), calls=%async_computation.23 | async-start | bytes 8388608
  392.4 4.8 slice-start.1
  402.0 1.5 copy-start.13
  403.4 157.6 %reduce-scatter.23.cloned.1.call-start = ((), (), s32[]{:S(2)}) async-start(), calls=%async_computation.22 | async-start | bytes 1572864 | tf_op jit(solution)/shard_map/reduce_scatter | solution.py:45
  406.6 6.3 %copy-start.10 = (bf16[1024,512]{1,0:T(8,128)(2,1)S(1)}, bf16[1024,512]{1,0:T(8,128)(2,1)}, u32[]{:S(2)}) copy-start(bf16[1024,512]{1,0:T(8,128)(2,1)} %all-gather.18.cloned.1.call-done) | copy-start | bytes 3145732
  427.6 6.3 %copy-start.24 = (bf16[1024,512]{0,1:T(8,128)(2,1)S(1)}, bf16[1024,512]{0,1:T(8,128)(2,1)}, u32[]{:S(2)}) copy-start(bf16[1024,512]{0,1:T(8,128)(2,1)} %all-gather.8.cloned.1.call-done) | copy-start | bytes 3145732
  431.4 4.1 copy-start.11
  542.2 4.4 copy-start.3
  556.2 7.0 %copy-start.1 = (bf16[2048,512]{1,0:T(8,128)(2,1)S(1)}, bf16[2048,512]{1,0:T(8,128)(2,1)}, u32[]{:S(2)}) copy-start(bf16[2048,512]{1,0:T(8,128)(2,1)} %param.25) | copy-start | bytes 6291460
  556.2 4.8 copy-start.9
Sparse Core Ops, SparseCore 0:
  13.7 19.5 reduce-scatter.8
  47.1 13.0 all-gather.7
  63.4 24.1 reduce-scatter.10
  93.8 24.7 all-gather.9
  126.3 20.5 reduce-scatter.12
  158.6 17.7 all-gather.11
  182.0 24.1 reduce-scatter.14
  218.6 24.7 all-gather.13
  250.4 20.4 reduce-scatter.16
  277.7 17.7 all-gather.15
  301.8 24.1 reduce-scatter.18
  344.4 24.7 all-gather.17
  372.7 13.1 reduce-scatter.20
  403.6 16.2 all-gather.19
  427.7 24.1 reduce-scatter.22

commit v2 on v1

v2 whole, which is shorter than its diff:
```python
import jax
import jax.numpy as jnp
from jax import lax
from jax.experimental import pallas as pl
from jax.experimental.pallas import tpu as pltpu
from jax.sharding import PartitionSpec as P

EPSILON = 1e-05
NEGATIVE = -1000000000.0
MESH = pl.DeviceIdType.MESH
BF = jnp.bfloat16
F32 = jnp.float32
PACK = 512


def partner_table():
    dp = lax.axis_index("dp")
    z, y, xh = dp // 8, (dp // 2) % 4, dp % 2
    wide, narrow = lax.axis_index("wide"), lax.axis_index("narrow")

    def at(z, y, xh):
        return (z * 8 + y * 2 + xh, wide, narrow)

    def parity(v):
        return (v % 2 + v // 2) % 2

    return {
        "y1": (at(z, y + 1 - 2 * (y % 2), xh), parity(y)),
        "z1": (at(z + 1 - 2 * (z % 2), y, xh), parity(z)),
        "y3": (at(z, 3 - y, xh), y // 2),
        "z3": (at(3 - z, y, xh), z // 2),
        "xh": (at(z, y, 1 - xh), xh),
        "wide": ((dp, 1 - wide, narrow), wide),
    }


ORDERS = (
    ("y1", "z1", "y3", "z3"),
    ("z1", "y3", "z3", "y1"),
    ("y3", "z3", "y1", "z1"),
    ("z3", "y1", "z1", "y3"),
)
SMALL_ORDER = ("wide", "y1", "z1", "y3", "z3", "xh")


class Summing:
    def __init__(self, buf, recv, out, send_sem, recv_sem, base, rows, recv_base, table):
        self.buf, self.recv, self.out = buf, recv, out
        self.send_sem, self.recv_sem, self.table = send_sem, recv_sem, table
        self.quarter = rows // 4
        self.offsets, self.places = [], []
        place = recv_base
        for q, order in enumerate(ORDERS):
            offset, size = base + q * self.quarter, self.quarter
            trail, slots = [offset], []
            for name in order:
                size = size // 2
                offset = pl.multiple_of(offset + table[name][1] * size, 16)
                trail.append(offset)
                slots.append(place)
                place += size
            slots.append(place)
            place += size
            self.offsets.append(trail)
            self.places.append(slots)
        self.sent = []

    def size(self, level):
        return self.quarter >> level

    def copy(self, q, step, src, dst, name):
        return pltpu.make_async_remote_copy(
            src_ref=src,
            dst_ref=dst,
            send_sem=self.send_sem.at[q, step],
            recv_sem=self.recv_sem.at[q, step],
            device_id=self.table[name][0],
            device_id_type=MESH,
        )

    def make(self, q, step):
        if step < 4:
            name, size = ORDERS[q][step], self.size(step + 1)
            start = self.offsets[q][step] + (1 - self.table[name][1]) * size
            src = self.buf.at[pl.ds(pl.multiple_of(start, 16), size), :]
            dst = self.recv.at[pl.ds(self.places[q][step], size), :]
        elif step == 4:
            name, size = "xh", self.size(4)
            src = self.buf.at[pl.ds(self.offsets[q][4], size), :]
            dst = self.recv.at[pl.ds(self.places[q][4], size), :]
        else:
            level = 9 - step
            name, size = ORDERS[q][level - 1], self.size(level)
            src = self.out.at[pl.ds(self.offsets[q][level], size), :]
            dst = src
        return self.copy(q, step, src, dst, name)

    def begin(self, q, step):
        copy = self.make(q, step)
        copy.start()
        self.sent.append(copy)

    def take(self, q, step):
        self.make(q, step).wait_recv()
        if step <= 4:
            level = min(step + 1, 4)
            size = self.size(level)
            target = self.out if step == 4 else self.buf
            chunk = 32
            offset, place = self.offsets[q][level], self.places[q][step]

            def add(i, carry):
                here = pl.ds(pl.multiple_of(offset + i * chunk, 16), chunk)
                there = pl.ds(pl.multiple_of(place + i * chunk, 16), chunk)
                total = self.buf[here, :].astype(F32) + self.recv[there, :].astype(F32)
                target[here, :] = total.astype(BF)
                return carry

            lax.fori_loop(0, size // chunk, add, 0)

    def open(self):
        for q in range(4):
            self.begin(q, 0)

    def advance(self, step):
        for q in range(4):
            self.take(q, step)
            if step < 8:
                self.begin(q, step + 1)

    def close(self):
        for copy in self.sent:
            copy.wait_send()


def sum_kernel(buf_in, small_in, out, small_out, buf, recv, small_recv, ss, rs, small_ss, small_rs):
    table = partner_table()
    barrier = pltpu.get_barrier_semaphore()
    for device, _ in table.values():
        pl.semaphore_signal(barrier, inc=1, device_id=device, device_id_type=MESH)
    pl.semaphore_wait(barrier, len(table))
    rows = buf_in.shape[0]
    work = Summing(buf_in, recv, out, ss, rs, 0, rows, 0, table)
    work.buf = buf
    chunk = 64

    def stage(i, carry):
        here = pl.ds(pl.multiple_of(i * chunk, 16), chunk)
        buf[here, :] = buf_in[here, :]
        return carry

    lax.fori_loop(0, rows // chunk, stage, 0)
    work.open()
    small_sent = []
    held = small_in[...]
    for step in range(9):
        if step < len(SMALL_ORDER):
            small_out[step] = held
            first = 24 if step == 0 else 0
            copy = pltpu.make_async_remote_copy(
                src_ref=small_out.at[step, pl.ds(first, 32 - first)],
                dst_ref=small_recv.at[step, pl.ds(first, 32 - first)],
                send_sem=small_ss.at[step],
                recv_sem=small_rs.at[step],
                device_id=table[SMALL_ORDER[step]][0],
                device_id_type=MESH,
            )
            copy.start()
            small_sent.append(copy)
        work.advance(step)
        if step < len(SMALL_ORDER):
            copy.wait_recv()
            if step == 0:
                top = held[:24]
                held = jnp.concatenate([top, held[24:] + small_recv[0, 24:, :]], 0)
            else:
                held = held + small_recv[step]
    small_out[len(SMALL_ORDER)] = held
    work.close()
    for copy in small_sent:
        copy.wait_send()


def sum_over_dp(packed, small):
    rows = packed.shape[0]
    steps = len(SMALL_ORDER)
    vmem = pl.BlockSpec(memory_space=pltpu.VMEM)
    out, small_out = pl.pallas_call(
        sum_kernel,
        out_shape=(
            jax.ShapeDtypeStruct((rows, PACK), BF),
            jax.ShapeDtypeStruct((steps + 1, 32, 256), F32),
        ),
        in_specs=[vmem, vmem],
        out_specs=(vmem, vmem),
        scratch_shapes=[
            pltpu.VMEM((rows, PACK), BF),
            pltpu.VMEM((rows, PACK), BF),
            pltpu.VMEM((steps, 32, 256), F32),
            pltpu.SemaphoreType.DMA((4, 9)),
            pltpu.SemaphoreType.DMA((4, 9)),
            pltpu.SemaphoreType.DMA((steps,)),
            pltpu.SemaphoreType.DMA((steps,)),
        ],
        compiler_params=pltpu.CompilerParams(
            collective_id=1, has_side_effects=True, vmem_limit_bytes=56 * 2**20
        ),
    )(packed, small)
    return out, small_out[steps]


SEQ = 512
PART = 256
ROWS_SMALL = 32
SMALL_QKV, SMALL_UP, SMALL_OUT, SMALL_DOWN, SMALL_NORM = 0, 6, 14, 16, 24
HALF_ROOT = 0.7071067811865476
INV_ROOT_2PI = 0.3989422804014327
QKV_ROWS, OUT_ROWS, UP_ROWS, DOWN_ROWS = 1536, 512, 2048, 2048
PACKED_ROWS = QKV_ROWS + OUT_ROWS + UP_ROWS + DOWN_ROWS
UP_BASE, DOWN_BASE, QKV_BASE, OUT_BASE = 0, 2048, 4096, 5632


def mm(a, b):
    return lax.dot_general(a, b, (((1,), (0,)), ((), ())), preferred_element_type=F32)


def mm_right(a, b):
    return lax.dot_general(a, b, (((1,), (1,)), ((), ())), preferred_element_type=F32)


def mm_left(a, b):
    return lax.dot_general(a, b, (((0,), (0,)), ((), ())), preferred_element_type=F32)


def span(start, size, step=128):
    return pl.ds(pl.multiple_of(start, step), size)


def tiles(count, body):
    lax.fori_loop(0, count, lambda i, carry: (body(i), carry)[1], 0)


class Net:
    def __init__(self, send_sem, recv_sem):
        self.send_sem, self.recv_sem, self.sent = send_sem, recv_sem, []

    def send(self, src, dst, device):
        i = len(self.sent)
        copy = pltpu.make_async_remote_copy(
            src_ref=src,
            dst_ref=dst,
            send_sem=self.send_sem.at[i],
            recv_sem=self.recv_sem.at[i],
            device_id=device,
            device_id_type=MESH,
        )
        copy.start()
        self.sent.append(copy)
        return copy

    def close(self):
        for copy in self.sent:
            copy.wait_send()


MESSAGES = 64


def layer_kernel(
    hid, seg_row, seg_col, qkv_w, qv_b, out_w, out_b, gain1, shift1, up_w, up_b, dn_w, dn_b,
    gain2, shift2, dy,
    hid_out, in_grad, packed, small,
    hid_o, qkvw_o, outw_o, upw_o, dnw_o,
    qs, ks, vs, probs, ctx_own, ctx_o,
    rs_send, rs_recv, stat_send, stat_recv,
    acc, res1, res2, inv1, pre,
    mixed_own, mixed_o, act_own, act_o, slope, gd_own, gd_o, gu_own, gu_o, ga_own, ga_o,
    dctx, dqkv_own, dqkv_o,
    send_sem, recv_sem,
):
    dp, w, n = lax.axis_index("dp"), lax.axis_index("wide"), lax.axis_index("narrow")
    twin, peer = (dp, w, 1 - n), (dp, 1 - w, n)
    barrier = pltpu.get_barrier_semaphore()
    for device in (twin, peer):
        pl.semaphore_signal(barrier, inc=1, device_id=device, device_id_type=MESH)
    pl.semaphore_wait(barrier, 2)
    net = Net(send_sem, recv_sem)
    seq_of = (w, 1 - w)
    base_of = (w * SEQ, (1 - w) * SEQ)
    lane = lax.broadcasted_iota(jnp.int32, (1, 128), 1)
    low = lane < 64
    picks = (low.astype(F32).astype(BF), (lane >= 64).astype(F32).astype(BF))
    scale = 0.125
    width = hid.shape[1]
    features = 2.0 * width

    hid_got = [None, None]
    hid_got[1] = net.send(hid.at[span(base_of[1], SEQ)], hid_o.at[1], twin)
    qkvw_got = net.send(qkv_w.at[:, span((1 - n) * 768, 768)], qkvw_o, twin)
    hid_got[0] = net.send(hid.at[span(base_of[0], SEQ)], hid_o.at[0], twin)
    upw_got = net.send(up_w.at[:, span((1 - n) * 1024, 1024)], upw_o, twin)
    dnw_got = net.send(dn_w.at[span((1 - n) * 1024, 1024), :], dnw_o, twin)
    outw_got = net.send(out_w.at[span((1 - n) * 256, 256), :], outw_o, twin)

    small[...] = jnp.zeros_like(small)

    def project(s):
        def block(i):
            p, r = i // 2, i % 2
            here = span(r * PART, PART)
            got = mm(hid[span(base_of[s] + r * PART, PART), :], qkv_w[:, span(n * 768 + p * 384, 384)])
            got += mm(hid_o[s, here, :], qkvw_o[:, span(p * 384, 384)])
            b0, b1, b2 = got[:, :128], got[:, 128:256], got[:, 256:]
            first, second = qv_b[pl.ds(n * 4 + 2 * p, 1), :], qv_b[pl.ds(n * 4 + 2 * p + 1, 1), :]
            q_bias = jnp.where(low, first, pltpu.roll(second, 64, 1))
            v_bias = jnp.where(low, pltpu.roll(first, 64, 1), second)
            qs[s, p, here, :] = (jnp.where(low, b0, b1) + q_bias).astype(BF)
            ks[s, p, here, :] = jnp.where(low, pltpu.roll(b0, 64, 1), pltpu.roll(b2, 64, 1)).astype(BF)
            vs[s, p, here, :] = (jnp.where(low, b1, b2) + v_bias).astype(BF)

        tiles(4, block)

    def attend_forward(s):
        def block(i):
            p, r = i // 2, i % 2
            here = span(r * PART, PART)
            q, k, v = qs[s, p, here, :], ks[s, p], vs[s, p]
            same = seg_col[span(base_of[s] + r * PART, PART), :] == seg_row[pl.ds(seq_of[s], 1), :]
            parts = []
            for h in range(2):
                score = jnp.where(same, mm_right(q * picks[h], k) * scale, NEGATIVE)
                raised = jnp.exp(score - jnp.max(score, -1, keepdims=True))
                weight = (raised / jnp.sum(raised, -1, keepdims=True)).astype(BF)
                probs[s, p * 2 + h, here, :] = weight
                parts.append(mm(weight, v))
            ctx_own[s, here, span(p * 128, 128)] = jnp.where(low, parts[0], parts[1]).astype(BF)

        tiles(4, block)
        return net.send(ctx_own.at[s], ctx_o.at[s], twin)

    def out_rows(s, c):
        here = pl.ds(c * PART, PART)
        return mm(ctx_own[s, here, :], out_w[span(n * 256, 256), :]) + mm(
            ctx_o[s, here, :], out_w[span((1 - n) * 256, 256), :]
        )

    def reduce_send(k, c, rows):
        here = pl.ds(c * PART, PART)
        rs_send[k, here, :] = rows.astype(BF)
        return net.send(rs_send.at[k, here], rs_recv.at[k, here], peer)

    def stat_pack(values):
        values = list(values) + [values[-1]] * (4 - len(values))
        return jnp.where(
            lane < 64,
            jnp.where(lane < 32, values[0], values[1]),
            jnp.where(lane < 96, values[2], values[3]),
        )

    def stat_exchange(k, c):
        here = pl.ds(c * PART, PART)
        return net.send(stat_send.at[k, here], stat_recv.at[k, here], twin)

    def stat_total(k, rows, i):
        return stat_send[k, rows, 32 * i : 32 * i + 1] + stat_recv[k, rows, 32 * i : 32 * i + 1]

    def row_sum(values):
        return jnp.sum(values, -1, keepdims=True)

    def column_add(row, values):
        for j in range(2):
            small[row + j : row + j + 1, :] += jnp.sum(
                values[:, j * 256 : (j + 1) * 256], 0, keepdims=True
            )

    STEP = 64

    def spread(own, c):
        here = pl.ds(c * PART, PART)
        across = net.send(own[0].at[0, here], own[0].at[1, here], peer)
        beside = net.send(own[0].at[0, here], own[1].at[0, here], twin)
        return across, beside

    def pass_on(own, c, across):
        here = pl.ds(c * PART, PART)
        across.wait_recv()
        return net.send(own[0].at[1, here], own[1].at[1, here], twin)

    hid_got[1].wait_recv()
    qkvw_got.wait_recv()
    project(1)
    ctx_got1 = attend_forward(1)
    hid_got[0].wait_recv()
    project(0)
    ctx_got1.wait_recv()
    rs1 = [reduce_send(0, c, out_rows(1, c)) for c in range(2)]
    ctx_got0 = attend_forward(0)
    ctx_got0.wait_recv()
    for c in range(2):
        acc[pl.ds(c * PART, PART), :] = out_rows(0, c)

    stats1 = []
    for c in range(2):
        rs1[c].wait_recv()

        def gather(i):
            rows = span(c * PART + i * STEP, STEP, 64)
            r = hid[span(base_of[0] + c * PART + i * STEP, STEP, 64), :].astype(F32)
            r = r + acc[rows, :] + rs_recv[0, rows, :].astype(F32) + out_b[...]
            res1[rows, :] = r
            stat_send[0, rows, :] = stat_pack([row_sum(r), row_sum(r * r)])

        tiles(PART // STEP, gather)
        stats1.append(stat_exchange(0, c))
    mixed = (mixed_own, mixed_o)
    mixed_sent = []
    for c in range(2):
        stats1[c].wait_recv()

        def normalize(i):
            rows = span(c * PART + i * STEP, STEP, 64)
            center = stat_total(0, rows, 0) / features
            inverse = lax.rsqrt(stat_total(0, rows, 1) / features - center * center + EPSILON)
            normed = (res1[rows, :] - center) * inverse
            res1[rows, :] = normed
            inv1[rows, :] = jnp.broadcast_to(inverse, (STEP, 128))
            mixed_own[0, rows, :] = (normed * gain1[...] + shift1[...]).astype(BF)

        tiles(PART // STEP, normalize)
        mixed_sent.append(spread(mixed, c))

    upw_got.wait_recv()

    def expand(s, c):
        here = pl.ds(c * PART, PART)
        pre[...] = mm(mixed_own[s, here, :], up_w[:, span(n * 1024, 1024)]) + mm(
            mixed_o[s, here, :], upw_o[...]
        )

        def bend(i):
            rows = span(i * 32, 32, 32)
            there = span(c * PART + i * 32, 32, 32)
            u = pre[rows, :] + up_b[:, span(n * 1024, 1024)]
            share = 0.5 * (1.0 + lax.erf(u * HALF_ROOT))
            act_own[s, there, :] = (u * share).astype(BF)
            slope[s, there, :] = (share + u * (INV_ROOT_2PI * jnp.exp(-0.5 * u * u))).astype(BF)

        tiles(PART // 32, bend)
        return net.send(act_own.at[s, here], act_o.at[s, here], twin)

    act_got = {}
    for c in range(2):
        mixed_sent[c][1].wait_recv()
        act_got[0, c] = expand(0, c)
    for c in range(2):
        pass_on(mixed, c, mixed_sent[c][0]).wait_recv()
        act_got[1, c] = expand(1, c)

    def contract_rows(s, c):
        here = pl.ds(c * PART, PART)
        return mm(act_own[s, here, :], dn_w[span(n * 1024, 1024), :]) + mm(
            act_o[s, here, :], dn_w[span((1 - n) * 1024, 1024), :]
        )

    rs2 = []
    for c in range(2):
        act_got[1, c].wait_recv()
        rs2.append(reduce_send(1, c, contract_rows(1, c)))
    for c in range(2):
        act_got[0, c].wait_recv()
        acc[pl.ds(c * PART, PART), :] = contract_rows(0, c)

    stats2 = []
    for c in range(2):
        rs2[c].wait_recv()

        def gather(i):
            rows = span(c * PART + i * STEP, STEP, 64)
            r = res1[rows, :] * gain1[...] + shift1[...]
            r = r + acc[rows, :] + rs_recv[1, rows, :].astype(F32) + dn_b[...]
            res2[rows, :] = r
            e = dy[rows, :].astype(F32) * gain2[...]
            stat_send[1, rows, :] = stat_pack(
                [row_sum(r), row_sum(r * r), row_sum(e), row_sum(e * r)]
            )

        tiles(PART // STEP, gather)
        stats2.append(stat_exchange(1, c))
    grad_down = (gd_own, gd_o)
    gd_sent = []
    for c in range(2):
        stats2[c].wait_recv()

        def normalize(i):
            rows = span(c * PART + i * STEP, STEP, 64)
            center = stat_total(1, rows, 0) / features
            inverse = lax.rsqrt(stat_total(1, rows, 1) / features - center * center + EPSILON)
            normed = (res2[rows, :] - center) * inverse
            hid_out[rows, :] = (normed * gain2[...] + shift2[...]).astype(BF)
            d = dy[rows, :].astype(F32)
            e = d * gain2[...]
            total = stat_total(1, rows, 2)
            cross = inverse * (stat_total(1, rows, 3) - center * total)
            grad = inverse * (e - total / features - normed * (cross / features))
            res2[rows, :] = grad
            gd_own[0, rows, :] = grad.astype(BF)
            column_add(SMALL_NORM + 4, d * normed)
            column_add(SMALL_NORM + 6, d)

        tiles(PART // STEP, normalize)
        gd_sent.append(spread(grad_down, c))

    dnw_got.wait_recv()

    def shrink_back(s, c):
        here = pl.ds(c * PART, PART)
        pre[...] = mm_right(gd_own[s, here, :], dn_w[span(n * 1024, 1024), :]) + mm_right(
            gd_o[s, here, :], dnw_o[...]
        )

        def bend(i):
            rows = span(i * 32, 32, 32)
            there = span(c * PART + i * 32, 32, 32)
            gu_own[s, there, :] = (pre[rows, :] * slope[s, there, :].astype(F32)).astype(BF)

        tiles(PART // 32, bend)
        return net.send(gu_own.at[s, here], gu_o.at[s, here], twin)

    gu_got = {}
    for c in range(2):
        gd_sent[c][1].wait_recv()
        gu_got[0, c] = shrink_back(0, c)
    for c in range(2):
        pass_on(grad_down, c, gd_sent[c][0]).wait_recv()
        gu_got[1, c] = shrink_back(1, c)

    def mixed_back(s, c):
        here = pl.ds(c * PART, PART)
        return mm_right(gu_own[s, here, :], up_w[:, span(n * 1024, 1024)]) + mm_right(
            gu_o[s, here, :], up_w[:, span((1 - n) * 1024, 1024)]
        )

    rs3 = []
    for c in range(2):
        gu_got[1, c].wait_recv()
        rs3.append(reduce_send(2, c, mixed_back(1, c)))
    for c in range(2):
        gu_got[0, c].wait_recv()
        acc[pl.ds(c * PART, PART), :] = mixed_back(0, c)

    def feed_forward_grads():
        for part, (a, g) in enumerate(((act_own, gu_own), (act_o, gu_o))):
            side = n if part == 0 else 1 - n

            def down_block(i):
                cols = span(i * 256, 256)
                got = mm_left(a[0, :, cols], gd_own[0]) + mm_left(a[1, :, cols], gd_own[1])
                packed[span(DOWN_BASE + side * 1024 + i * 256, 256), :] = got.astype(BF)

            tiles(4, down_block)

            def up_block(i):
                j, r = i % 2, i // 2
                cols, where = span(j * 512, 512), span(r * 256, 256)
                got = mm_left(mixed_own[0, :, where], g[0, :, cols]) + mm_left(
                    mixed_own[1, :, where], g[1, :, cols]
                )
                packed[span(UP_BASE + (side * 2 + j) * 512 + r * 256, 256), :] = got.astype(BF)

            tiles(4, up_block)

            def up_bias(i):
                cols = span(i * 256, 256)
                total = jnp.sum(g[0, :, cols].astype(F32), 0, keepdims=True) + jnp.sum(
                    g[1, :, cols].astype(F32), 0, keepdims=True
                )
                small[pl.ds(SMALL_UP + side * 4 + i, 1), :] = total

            tiles(4, up_bias)
        for s in range(2):
            column_add(SMALL_DOWN, gd_own[s].astype(F32))

    feed_forward_grads()

    stats3 = []
    for c in range(2):
        rs3[c].wait_recv()

        def gather(i):
            rows = span(c * PART + i * STEP, STEP, 64)
            g = res2[rows, :] + acc[rows, :] + rs_recv[2, rows, :].astype(F32)
            res2[rows, :] = g
            e = g * gain1[...]
            n1 = res1[rows, :]
            stat_send[2, rows, :] = stat_pack([row_sum(e), row_sum(e * n1)])
            column_add(SMALL_NORM, g * n1)
            column_add(SMALL_NORM + 2, g)

        tiles(PART // STEP, gather)
        stats3.append(stat_exchange(2, c))
    grad_attn = (ga_own, ga_o)
    ga_sent = []
    for c in range(2):
        stats3[c].wait_recv()

        def normalize(i):
            rows = span(c * PART + i * STEP, STEP, 64)
            e = res2[rows, :] * gain1[...]
            inverse = inv1[rows, 0:1]
            grad = inverse * (
                e
                - stat_total(2, rows, 0) / features
                - res1[rows, :] * (stat_total(2, rows, 1) / features)
            )
            res2[rows, :] = grad
            ga_own[0, rows, :] = grad.astype(BF)

        tiles(PART // STEP, normalize)
        ga_sent.append(spread(grad_attn, c))

    outw_got.wait_recv()

    def attend_back(s):
        dctx[...] = (
            mm_right(ga_own[s], out_w[span(n * 256, 256), :]) + mm_right(ga_o[s], outw_o[...])
        ).astype(BF)

        def block(p):
            q, k, v, d = qs[s, p], ks[s, p], vs[s, p], dctx[:, span(p * 128, 128)]
            dq, dk, dv = [], [], []
            for h in range(2):
                weight = probs[s, p * 2 + h]
                wide_weight = weight.astype(F32)
                dprob = mm_right(d * picks[h], v)
                inner = jnp.sum(dprob * wide_weight, -1, keepdims=True)
                dscore = (wide_weight * (dprob - inner)).astype(BF)
                dq.append(mm(dscore, k))
                dk.append(mm_left(dscore, q))
                dv.append(mm_left(weight, d))
            dqs = jnp.where(low, dq[0], dq[1]) * scale
            dks = pltpu.roll(jnp.where(low, dk[0], dk[1]) * scale, 64, 1)
            dvs = jnp.where(low, dv[0], dv[1])
            dqkv_own[s, :, span(p * 384, 128)] = jnp.where(low, dqs, dks).astype(BF)
            dqkv_own[s, :, span(p * 384 + 128, 128)] = jnp.where(low, dvs, dqs).astype(BF)
            dqkv_own[s, :, span(p * 384 + 256, 128)] = jnp.where(low, dks, dvs).astype(BF)

        tiles(2, block)
        return net.send(dqkv_own.at[s], dqkv_o.at[s], twin)

    for c in range(2):
        ga_sent[c][1].wait_recv()
    dqkv_got = [attend_back(0), None]
    ga_passed = [pass_on(grad_attn, c, ga_sent[c][0]) for c in range(2)]
    for copy in ga_passed:
        copy.wait_recv()
    dqkv_got[1] = attend_back(1)

    for part, ctx in enumerate((ctx_own, ctx_o)):
        side = n if part == 0 else 1 - n
        got = mm_left(ctx[0], ga_own[0]) + mm_left(ctx[1], ga_own[1])
        packed[span(OUT_BASE + side * 256, 256), :] = got.astype(BF)
    for s in range(2):
        column_add(SMALL_OUT, ga_own[s].astype(F32))

    def input_rows(s, c):
        here = pl.ds(c * PART, PART)
        return mm_right(dqkv_own[s, here, :], qkv_w[:, span(n * 768, 768)]) + mm_right(
            dqkv_o[s, here, :], qkv_w[:, span((1 - n) * 768, 768)]
        )

    dqkv_got[1].wait_recv()
    rs4 = [reduce_send(3, c, input_rows(1, c)) for c in range(2)]
    dqkv_got[0].wait_recv()
    for c in range(2):
        acc[pl.ds(c * PART, PART), :] = input_rows(0, c)

    for part, g in enumerate((dqkv_own, dqkv_o)):
        side = n if part == 0 else 1 - n

        def qkv_block(i):
            j, r = i // 2, i % 2
            cols, where = span(j * 256, 256), span(r * 256, 256)
            got = mm_left(hid[span(base_of[0], SEQ), where], g[0, :, cols]) + mm_left(
                hid[span(base_of[1], SEQ), where], g[1, :, cols]
            )
            at = side * 3 + j
            packed[
                span(QKV_BASE + (at // 2) * 512 + r * 256, 256), span((at % 2) * 256, 256)
            ] = got.astype(BF)

        tiles(6, qkv_block)

        def qkv_bias(j):
            cols = span(j * 256, 256)
            total = jnp.sum(g[0, :, cols].astype(F32), 0, keepdims=True) + jnp.sum(
                g[1, :, cols].astype(F32), 0, keepdims=True
            )
            small[pl.ds(SMALL_QKV + side * 3 + j, 1), :] = total

        tiles(3, qkv_bias)

    for c in range(2):
        rs4[c].wait_recv()

        def finish(i):
            rows = span(c * PART + i * STEP, STEP, 64)
            in_grad[rows, :] = res2[rows, :] + acc[rows, :] + rs_recv[3, rows, :].astype(F32)

        tiles(PART // STEP, finish)
    net.close()


def layer_call(*arrays):
    vmem = pl.BlockSpec(memory_space=pltpu.VMEM)
    shapes = [
        ((2, SEQ, 512), BF), ((512, 768), BF), ((256, 512), BF), ((512, 1024), BF), ((1024, 512), BF),
        ((2, 2, SEQ, 128), BF), ((2, 2, SEQ, 128), BF), ((2, 2, SEQ, 128), BF),
        ((2, 4, SEQ, SEQ), BF), ((2, SEQ, 256), BF), ((2, SEQ, 256), BF),
        ((4, SEQ, 512), BF), ((4, SEQ, 512), BF), ((3, SEQ, 128), F32), ((3, SEQ, 128), F32),
        ((SEQ, 512), F32), ((SEQ, 512), F32), ((SEQ, 512), F32), ((SEQ, 128), F32), ((PART, 1024), F32),
        ((2, SEQ, 512), BF), ((2, SEQ, 512), BF), ((2, SEQ, 1024), BF), ((2, SEQ, 1024), BF),
        ((2, SEQ, 1024), BF), ((2, SEQ, 512), BF), ((2, SEQ, 512), BF), ((2, SEQ, 1024), BF),
        ((2, SEQ, 1024), BF), ((2, SEQ, 512), BF), ((2, SEQ, 512), BF),
        ((SEQ, 256), BF), ((2, SEQ, 768), BF), ((2, SEQ, 768), BF),
    ]
    return pl.pallas_call(
        layer_kernel,
        out_shape=(
            jax.ShapeDtypeStruct((SEQ, 512), BF),
            jax.ShapeDtypeStruct((SEQ, 512), F32),
            jax.ShapeDtypeStruct((PACKED_ROWS, PACK), BF),
            jax.ShapeDtypeStruct((ROWS_SMALL, 256), F32),
        ),
        in_specs=[vmem] * len(arrays),
        out_specs=(vmem,) * 4,
        scratch_shapes=[pltpu.VMEM(*shape) for shape in shapes]
        + [pltpu.SemaphoreType.DMA((MESSAGES,)), pltpu.SemaphoreType.DMA((MESSAGES,))],
        compiler_params=pltpu.CompilerParams(
            collective_id=2, has_side_effects=True, vmem_limit_bytes=60 * 2**20
        ),
    )(*arrays)


def per_device(
    hidden_in,
    segment_ids,
    qkv_weight,
    qv_bias,
    out_weight,
    out_bias,
    norm1_gain,
    norm1_shift,
    up_weight,
    up_bias,
    down_weight,
    down_bias,
    norm2_gain,
    norm2_shift,
    out_grad,
):
    half_width = hidden_in.shape[1]
    heads_here, head_width = qkv_weight.shape[1], qkv_weight.shape[3]
    hidden_out, input_grad, packed, small = layer_call(
        hidden_in,
        segment_ids.reshape(2, SEQ),
        segment_ids.reshape(-1, 1),
        qkv_weight.reshape(half_width, -1),
        qv_bias.reshape(heads_here, -1),
        out_weight.reshape(-1, half_width),
        out_bias[None],
        norm1_gain[None],
        norm1_shift[None],
        up_weight,
        up_bias[None],
        down_weight,
        down_bias[None],
        norm2_gain[None],
        norm2_shift[None],
        out_grad,
    )
    total, small = sum_over_dp(packed, small)
    total = total.astype(F32)

    def columns(base, rows):
        return jnp.concatenate(
            [total[i : i + half_width] for i in range(base, base + rows, half_width)], 1
        )

    qkv_sums = small[SMALL_QKV : SMALL_QKV + 6].reshape(heads_here, 3, head_width)
    norms = small[SMALL_NORM : SMALL_NORM + 8].reshape(4, half_width)
    return (
        hidden_out,
        input_grad,
        columns(QKV_BASE, QKV_ROWS).reshape(half_width, heads_here, 3, head_width),
        jnp.stack([qkv_sums[:, 0], qkv_sums[:, 2]], 1),
        total[OUT_BASE : OUT_BASE + OUT_ROWS].reshape(heads_here, head_width, half_width),
        small[SMALL_OUT : SMALL_OUT + 2].reshape(-1),
        norms[0],
        norms[1],
        columns(UP_BASE, UP_ROWS),
        small[SMALL_UP : SMALL_UP + 8].reshape(-1),
        total[DOWN_BASE : DOWN_BASE + DOWN_ROWS],
        small[SMALL_DOWN : SMALL_DOWN + 2].reshape(-1),
        norms[2],
        norms[3],
    )


def solution(mesh):
    return jax.shard_map(
        per_device,
        mesh=mesh,
        in_specs=(
            P("dp", "narrow"),
            P("dp"),
            P("narrow", "wide", None, None),
            P("wide", None, None),
            P("wide", None, "narrow"),
            P("narrow"),
            P("narrow"),
            P("narrow"),
            P("narrow", "wide"),
            P("wide"),
            P("wide", "narrow"),
            P("narrow"),
            P("narrow"),
            P("narrow"),
            P(("dp", "wide"), "narrow"),
        ),
        out_specs=(
            P(("dp", "wide"), "narrow"),
            P(("dp", "wide"), "narrow"),
            P("narrow", "wide", None, None),
            P("wide", None, None),
            P("wide", None, "narrow"),
            P("narrow"),
            P("narrow"),
            P("narrow"),
            P("narrow", "wide"),
            P("wide"),
            P("wide", "narrow"),
            P("narrow"),
            P("narrow"),
            P("narrow"),
        ),
        check_vma=False,
    )
```

time: 573 us -> 254 us (0.44)
  waiting for transfers between devices: 276 us -> 0 us
  Pallas kernels: 93.5 us -> 223 us
  matrix products: 79.9 us -> 0 us
  other arithmetic: 53.2 us -> 3.2 us
  blocking collectives: 21.3 us -> 0 us
  between operations: 14.5 us -> 0.68 us
    reduce_scatter x8 -> x0, waiting for transfers between devices: 146 us -> none  [the longest x4 73 us: narrow_rows_sum(): return lax.psum_scatter(terms, 'narrow', scatter_dimension=0, tiled=True)]
    pallas_call x0 -> x1, Pallas kernels: none -> 130 us  [layer_call(): pl.pallas_call(layer_kernel, out_shape=(jax.ShapeDtypeStruct((SEQ, 512),...]
    all_gather x7 -> x0, waiting for transfers between devices: 130 us -> none  [the longest x3 74.7 us: wide_rows_gather(): return lax.all_gather(pieces, 'wide', axis=0, tiled=True)]
    dot_general x18 -> x0, matrix products: 79.9 us -> none  [the longest x10 47.5 us: contract(): lax.dot_general(left_side, right_side, (((left_dim,), (right_dim,)), ((),...]
    convert_element_type x7 -> x0, other arithmetic: 29.7 us -> none  [the longest x1 11.6 us: per_device(): activated_full = narrow_rows_gather(gelu_exact(upward).astype(jnp.bfloat16))]
    psum x4 -> x0, blocking collectives: 21.3 us -> none  [narrow_stats(): return lax.psum((first, second), 'narrow')]
    reduce_sum x9 -> x0, other arithmetic: 14.2 us -> none  [the longest x2 3.99 us: norm_forward(): jnp.sum(rows_in, -1)]
    reshape x4 -> x5, local copies, waits for them, and re-layouts: 0.86 us -> 7.01 us  [the longest x1 2.58 us: per_device(): qkv_weight.reshape(half_width, -1)]
  transfers between devices with their start and end apart: 15 -> 0, of which waited for: 14 -> 0; matrix products, arithmetic and copies ran while one was open for 9% -> 0% of each run, Pallas kernels for 16% -> 0%
where the time goes in v2:
time: 254 us; the launch traced here: 253 us
  Pallas kernels  223 us (88%)
  local copies, waits for them, and re-layouts  26.3 us (10%)
  other arithmetic  3.2 us (1%)
    pallas_call x1, Pallas kernels, layer_call(): pl.pallas_call(layer_kernel, out_shape=(jax.ShapeDtypeStruct((SEQ, 512),...  130 us
    pallas_call x1, Pallas kernels, sum_over_dp(): pl.pallas_call(sum_kernel, out_shape=(jax.ShapeDtypeStruct((rows, PACK),...  92.4 us
    unnamed x13, local copies, waits for them, and re-layouts  9.78 us

profile of v2, /device:TPU:0, one launch (start us, length us, event | category | flops | bytes accessed | tf_op | source)
XLA Modules:
  0.0 253.1 jit_solution(488673038342018307)
XLA Ops:
  0.6 1.4 reshape.83.qv_b
  2.0 1.3 reshape.80.seg_row
  3.3 1.7 copy.31.seg_col
  5.0 2.6 %copy.32.qkv_w = bf16[512,1536]{1,0:T(8,128)(2,1)} copy(bf16[512,1536]{0,1:T(8,128)(2,1)} %bitcast.34) | data formatting | bytes 3145728 | tf_op jit(solution)/shard_map/reshape | solution.py:767
  7.6 130.5 %shard_map.254 = (bf16[512,512]{1,0:T(8,128)(2,1)}, f32[512,512]{1,0:T(8,128)}, bf16[6144,512]{1,0:T(8,128)(2,1)}, f32[32,256]{1,0:T(8,128)}) custom-call(bf16[1024,512]{1,0:T(8,128)(2,1)} %hid.1, s32[2,512]{1,0:T(2,128)} %reshape.80.seg_row, s32[1024,1]{1,0:T(8,128)} %copy.31.seg_col, bf16[512,1536]{1,0:T(8,128)(2,1)} %copy.32.qkv_w, ...), custom_call_target="tpu_custom_call" | custom-call | tf_op jit(solution)/shard_map/pallas_call | solution.py:726
  138.0 92.4 %shard_map.255 = (bf16[6144,512]{1,0:T(8,128)(2,1)}, f32[7,32,256]{2,1,0:T(8,128)}) custom-call(bf16[6144,512]{1,0:T(8,128)(2,1)} %get-tuple-element.22.buf_in, f32[32,256]{1,0:T(8,128)} %get-tuple-element.23.small_in), custom_call_target="tpu_custom_call" | custom-call | tf_op jit(solution)/shard_map/pallas_call | solution.py:188
  230.5 0.7 slice_bitcast_fusion
  231.2 0.6 copy.37
  231.8 0.7 slice.80
  232.5 0.9 slice_bitcast_fusion.1
  233.4 0.6 copy.40
  233.9 0.6 copy.39
  234.5 0.6 copy.38
  235.1 0.6 copy.36
  235.7 0.6 copy.35
  236.3 0.6 copy.34
  236.8 0.1 reshape.86
  236.9 0.6 pad_maximum_fusion.2
  237.5 0.0 copy-start
  237.5 4.3 %slice.106 = f32[2048,512]{1,0:T(8,128)} slice(bf16[6144,512]{1,0:T(8,128)(2,1)} %get-tuple-element.24), slice={[2048:4096], [0:512]} | slice | bytes 8388608 | tf_op jit(solution)/shard_map/slice | solution.py:802
  241.9 0.0 copy-done
  241.9 2.1 fusion
  244.0 2.4 pad_maximum_fusion
  246.4 0.2 pad_maximum_fusion.1
  246.6 2.4 copy.33
  249.0 1.9 copy.43
  250.8 2.3 copy.44
  (1 shorter events, 0.0 us)
Async XLA Ops:
  237.5 4.4 %copy-start = (bf16[6144,512]{1,0:T(8,128)(2,1)S(1)}, bf16[6144,512]{1,0:T(8,128)(2,1)}, u32[]{:S(2)}) copy-start(bf16[6144,512]{1,0:T(8,128)(2,1)} %get-tuple-element.24) | copy-start | bytes 18874372

commit v3 on v2

--- a/solution.py
+++ b/solution.py
@@ -44,14 +44,14 @@
 
 
 class Summing:
-    def __init__(self, buf, recv, out, send_sem, recv_sem, base, rows, recv_base, table):
-        self.buf, self.recv, self.out = buf, recv, out
-        self.send_sem, self.recv_sem, self.table = send_sem, recv_sem, table
+    def __init__(self, buf, landing, fin, out, sems, base, rows, fin_base, table):
+        self.buf, self.landing, self.fin, self.out = buf, landing, fin, out
+        self.send_sem, self.recv_sem, self.local_sem = sems
+        self.table, self.fin_base = table, fin_base
         self.quarter = rows // 4
         self.offsets, self.places = [], []
-        place = recv_base
         for q, order in enumerate(ORDERS):
-            offset, size = base + q * self.quarter, self.quarter
+            offset, size, place = base + q * self.quarter, self.quarter, 0
             trail, slots = [offset], []
             for name in order:
                 size = size // 2
@@ -60,7 +60,6 @@
                 slots.append(place)
                 place += size
             slots.append(place)
-            place += size
             self.offsets.append(trail)
             self.places.append(slots)
         self.sent = []
@@ -68,7 +67,24 @@
     def size(self, level):
         return self.quarter >> level
 
-    def copy(self, q, step, src, dst, name):
+    def final(self, q):
+        return pl.ds(self.fin_base + q * self.size(4), self.size(4))
+
+    def make(self, q, step):
+        if step < 4:
+            name, size = ORDERS[q][step], self.size(step + 1)
+            start = self.offsets[q][step] + (1 - self.table[name][1]) * size
+            src = self.buf.at[pl.ds(pl.multiple_of(start, 16), size), :]
+            dst = self.landing(q, self.places[q][step], size)
+        elif step == 4:
+            name, size = "xh", self.size(4)
+            src = self.buf.at[pl.ds(self.offsets[q][4], size), :]
+            dst = self.landing(q, self.places[q][4], size)
+        else:
+            level = 9 - step
+            name, size = ORDERS[q][level - 1], self.size(level)
+            dst = self.out.at[pl.ds(self.offsets[q][level], size), :]
+            src = self.fin.at[self.final(q), :] if step == 5 else dst
         return pltpu.make_async_remote_copy(
             src_ref=src,
             dst_ref=dst,
@@ -78,22 +94,11 @@
             device_id_type=MESH,
         )
 
-    def make(self, q, step):
-        if step < 4:
-            name, size = ORDERS[q][step], self.size(step + 1)
-            start = self.offsets[q][step] + (1 - self.table[name][1]) * size
-            src = self.buf.at[pl.ds(pl.multiple_of(start, 16), size), :]
-            dst = self.recv.at[pl.ds(self.places[q][step], size), :]
-        elif step == 4:
-            name, size = "xh", self.size(4)
-            src = self.buf.at[pl.ds(self.offsets[q][4], size), :]
-            dst = self.recv.at[pl.ds(self.places[q][4], size), :]
-        else:
-            level = 9 - step
-            name, size = ORDERS[q][level - 1], self.size(level)
-            src = self.out.at[pl.ds(self.offsets[q][level], size), :]
-            dst = src
-        return self.copy(q, step, src, dst, name)
+    def keep(self, q):
+        where = pl.ds(self.offsets[q][4], self.size(4))
+        return pltpu.make_async_copy(
+            self.fin.at[self.final(q), :], self.out.at[where, :], self.local_sem.at[q]
+        )
 
     def begin(self, q, step):
         copy = self.make(q, step)
@@ -102,21 +107,25 @@
 
     def take(self, q, step):
         self.make(q, step).wait_recv()
-        if step <= 4:
-            level = min(step + 1, 4)
-            size = self.size(level)
-            target = self.out if step == 4 else self.buf
-            chunk = 32
-            offset, place = self.offsets[q][level], self.places[q][step]
-
-            def add(i, carry):
-                here = pl.ds(pl.multiple_of(offset + i * chunk, 16), chunk)
-                there = pl.ds(pl.multiple_of(place + i * chunk, 16), chunk)
-                total = self.buf[here, :].astype(F32) + self.recv[there, :].astype(F32)
-                target[here, :] = total.astype(BF)
-                return carry
-
-            lax.fori_loop(0, size // chunk, add, 0)
+        if step > 4:
+            return
+        size, chunk = self.size(min(step + 1, 4)), 32
+        offset, place = self.offsets[q][min(step + 1, 4)], self.places[q][step]
+
+        def add(i, carry):
+            here = pl.ds(pl.multiple_of(offset + i * chunk, 16), chunk)
+            there = self.landing(q, pl.multiple_of(place + i * chunk, 16), chunk)
+            total = (self.buf[here, :].astype(F32) + there[...].astype(F32)).astype(BF)
+            if step == 4:
+                first = self.fin_base + q * size
+                self.fin[pl.ds(pl.multiple_of(first + i * chunk, 16), chunk), :] = total
+            else:
+                self.buf[here, :] = total
+            return carry
+
+        lax.fori_loop(0, size // chunk, add, 0)
+        if step == 4:
+            self.keep(q).start()
 
     def open(self):
         for q in range(4):
@@ -125,6 +134,8 @@
     def advance(self, step):
         for q in range(4):
             self.take(q, step)
+            if step == 5:
+                self.keep(q).wait()
             if step < 8:
                 self.begin(q, step + 1)
 
@@ -133,80 +144,36 @@
             copy.wait_send()
 
 
-def sum_kernel(buf_in, small_in, out, small_out, buf, recv, small_recv, ss, rs, small_ss, small_rs):
-    table = partner_table()
-    barrier = pltpu.get_barrier_semaphore()
-    for device, _ in table.values():
-        pl.semaphore_signal(barrier, inc=1, device_id=device, device_id_type=MESH)
-    pl.semaphore_wait(barrier, len(table))
-    rows = buf_in.shape[0]
-    work = Summing(buf_in, recv, out, ss, rs, 0, rows, 0, table)
-    work.buf = buf
-    chunk = 64
-
-    def stage(i, carry):
-        here = pl.ds(pl.multiple_of(i * chunk, 16), chunk)
-        buf[here, :] = buf_in[here, :]
-        return carry
-
-    lax.fori_loop(0, rows // chunk, stage, 0)
-    work.open()
-    small_sent = []
-    held = small_in[...]
-    for step in range(9):
-        if step < len(SMALL_ORDER):
-            small_out[step] = held
-            first = 24 if step == 0 else 0
-            copy = pltpu.make_async_remote_copy(
-                src_ref=small_out.at[step, pl.ds(first, 32 - first)],
-                dst_ref=small_recv.at[step, pl.ds(first, 32 - first)],
-                send_sem=small_ss.at[step],
-                recv_sem=small_rs.at[step],
-                device_id=table[SMALL_ORDER[step]][0],
-                device_id_type=MESH,
-            )
-            copy.start()
-            small_sent.append(copy)
-        work.advance(step)
-        if step < len(SMALL_ORDER):
-            copy.wait_recv()
-            if step == 0:
-                top = held[:24]
-                held = jnp.concatenate([top, held[24:] + small_recv[0, 24:, :]], 0)
-            else:
-                held = held + small_recv[step]
-    small_out[len(SMALL_ORDER)] = held
-    work.close()
-    for copy in small_sent:
-        copy.wait_send()
-
-
-def sum_over_dp(packed, small):
-    rows = packed.shape[0]
-    steps = len(SMALL_ORDER)
-    vmem = pl.BlockSpec(memory_space=pltpu.VMEM)
-    out, small_out = pl.pallas_call(
-        sum_kernel,
-        out_shape=(
-            jax.ShapeDtypeStruct((rows, PACK), BF),
-            jax.ShapeDtypeStruct((steps + 1, 32, 256), F32),
-        ),
-        in_specs=[vmem, vmem],
-        out_specs=(vmem, vmem),
-        scratch_shapes=[
-            pltpu.VMEM((rows, PACK), BF),
-            pltpu.VMEM((rows, PACK), BF),
-            pltpu.VMEM((steps, 32, 256), F32),
-            pltpu.SemaphoreType.DMA((4, 9)),
-            pltpu.SemaphoreType.DMA((4, 9)),
-            pltpu.SemaphoreType.DMA((steps,)),
-            pltpu.SemaphoreType.DMA((steps,)),
-        ],
-        compiler_params=pltpu.CompilerParams(
-            collective_id=1, has_side_effects=True, vmem_limit_bytes=56 * 2**20
-        ),
-    )(packed, small)
-    return out, small_out[steps]
+class SmallSum:
+    def __init__(self, held, kept, recv, sems, table):
+        self.held, self.kept, self.recv, self.table = held, kept, recv, table
+        self.send_sem, self.recv_sem = sems
+        self.sent = []
+
+    def begin(self, step):
+        self.kept[step] = self.held[...]
+        first = 24 if step == 0 else 0
+        copy = pltpu.make_async_remote_copy(
+            src_ref=self.kept.at[step, pl.ds(first, ROWS_SMALL - first)],
+            dst_ref=self.recv.at[step, pl.ds(first, ROWS_SMALL - first)],
+            send_sem=self.send_sem.at[step],
+            recv_sem=self.recv_sem.at[step],
+            device_id=self.table[SMALL_ORDER[step]][0],
+            device_id_type=MESH,
+        )
+        copy.start()
+        self.sent.append(copy)
+
+    def take(self, step):
+        self.sent[step].wait_recv()
+        first = 24 if step == 0 else 0
+        self.held[first:, :] = self.held[first:, :] + self.recv[step, first:, :]
+        if step + 1 < len(SMALL_ORDER):
+            self.begin(step + 1)
+
+    def close(self):
+        for copy in self.sent:
+            copy.wait_send()
 
 
 SEQ = 512
@@ -242,7 +209,8 @@
 
 class Net:
     def __init__(self, send_sem, recv_sem):
-        self.send_sem, self.recv_sem, self.sent = send_sem, recv_sem, []
+        self.send_sem, self.recv_sem = send_sem, recv_sem
+        self.sent, self.drained = [], []
 
     def send(self, src, dst, device):
         i = len(self.sent)
@@ -258,32 +226,38 @@
         self.sent.append(copy)
         return copy
 
+    def drain(self, copies):
+        for copy in copies:
+            if not any(copy is done for done in self.drained):
+                copy.wait_send()
+                self.drained.append(copy)
+
     def close(self):
-        for copy in self.sent:
-            copy.wait_send()
+        self.drain(self.sent)
 
 
 MESSAGES = 64
 
 
 def layer_kernel(
-    hid, seg_row, seg_col, qkv_w, qv_b, out_w, out_b, gain1, shift1, up_w, up_b, dn_w, dn_b,
+    hid, seg, qkv_w, qv_b, out_w, out_b, gain1, shift1, up_w, up_b, dn_w, dn_b,
     gain2, shift2, dy,
-    hid_out, in_grad, packed, small,
+    hid_out, in_grad, out, small,
     hid_o, qkvw_o, outw_o, upw_o, dnw_o,
     qs, ks, vs, probs, ctx_own, ctx_o,
     rs_send, rs_recv, stat_send, stat_recv,
     acc, res1, res2, inv1, pre,
     mixed_own, mixed_o, act_own, act_o, slope, gd_own, gd_o, gu_own, gu_o, ga_own, ga_o,
-    dctx, dqkv_own, dqkv_o,
-    send_sem, recv_sem,
+    dctx, packed, landing1, fin, small_kept, small_recv,
+    send_sem, recv_sem, ss1, rs1_sem, ls1, ss2, rs2_sem, ls2, small_ss, small_rs,
 ):
     dp, w, n = lax.axis_index("dp"), lax.axis_index("wide"), lax.axis_index("narrow")
     twin, peer = (dp, w, 1 - n), (dp, 1 - w, n)
+    table = partner_table()
     barrier = pltpu.get_barrier_semaphore()
-    for device in (twin, peer):
+    for device in [twin] + [entry[0] for entry in table.values()]:
         pl.semaphore_signal(barrier, inc=1, device_id=device, device_id_type=MESH)
-    pl.semaphore_wait(barrier, 2)
+    pl.semaphore_wait(barrier, 1 + len(table))
     net = Net(send_sem, recv_sem)
     seq_of = (w, 1 - w)
     base_of = (w * SEQ, (1 - w) * SEQ)
@@ -311,21 +285,29 @@
             got = mm(hid[span(base_of[s] + r * PART, PART), :], qkv_w[:, span(n * 768 + p * 384, 384)])
             got += mm(hid_o[s, here, :], qkvw_o[:, span(p * 384, 384)])
             b0, b1, b2 = got[:, :128], got[:, 128:256], got[:, 256:]
-            first, second = qv_b[pl.ds(n * 4 + 2 * p, 1), :], qv_b[pl.ds(n * 4 + 2 * p + 1, 1), :]
-            q_bias = jnp.where(low, first, pltpu.roll(second, 64, 1))
-            v_bias = jnp.where(low, pltpu.roll(first, 64, 1), second)
+            head = n * 4 + 2 * p
+            q_bias, v_bias = [
+                jnp.concatenate([qv_b[head, i : i + 1, :], qv_b[head + 1, i : i + 1, :]], 1)
+                for i in range(2)
+            ]
             qs[s, p, here, :] = (jnp.where(low, b0, b1) + q_bias).astype(BF)
             ks[s, p, here, :] = jnp.where(low, pltpu.roll(b0, 64, 1), pltpu.roll(b2, 64, 1)).astype(BF)
             vs[s, p, here, :] = (jnp.where(low, b1, b2) + v_bias).astype(BF)
 
         tiles(4, block)
 
-    def attend_forward(s):
-        def block(i):
-            p, r = i // 2, i % 2
-            here = span(r * PART, PART)
+    def segments(s):
+        row = jnp.concatenate([seg[pl.ds(4 * seq_of[s] + i, 1), :] for i in range(4)], 1)
+        row = row.astype(F32)
+        return row, jnp.transpose(jnp.broadcast_to(row, (128, SEQ)))
+
+    def attend_forward(s, r):
+        here = pl.ds(r * PART, PART)
+        row, column = segments(s)
+        same = column[r * PART : (r + 1) * PART, 0:1] == row
+
+        def block(p):
             q, k, v = qs[s, p, here, :], ks[s, p], vs[s, p]
-            same = seg_col[span(base_of[s] + r * PART, PART), :] == seg_row[pl.ds(seq_of[s], 1), :]
             parts = []
             for h in range(2):
                 score = jnp.where(same, mm_right(q * picks[h], k) * scale, NEGATIVE)
@@ -335,8 +317,8 @@
                 parts.append(mm(weight, v))
             ctx_own[s, here, span(p * 128, 128)] = jnp.where(low, parts[0], parts[1]).astype(BF)
 
-        tiles(4, block)
-        return net.send(ctx_own.at[s], ctx_o.at[s], twin)
+        tiles(2, block)
+        return net.send(ctx_own.at[s, here], ctx_o.at[s, here], twin)
 
     def out_rows(s, c):
         here = pl.ds(c * PART, PART)
@@ -344,10 +326,15 @@
             ctx_o[s, here, :], out_w[span((1 - n) * 256, 256), :]
         )
 
+    rs_sent = {}
+
     def reduce_send(k, c, rows):
         here = pl.ds(c * PART, PART)
-        rs_send[k, here, :] = rows.astype(BF)
-        return net.send(rs_send.at[k, here], rs_recv.at[k, here], peer)
+        slot = k % 2
+        if k >= 2:
+            net.drain([rs_sent[k - 2, c]])
+        rs_send[slot, here, :] = rows.astype(BF)
+        rs_sent[k, c] = net.send(rs_send.at[slot, here], rs_recv.at[slot, here], peer)
 
     def stat_pack(values):
         values = list(values) + [values[-1]] * (4 - len(values))
@@ -389,19 +376,25 @@
     hid_got[1].wait_recv()
     qkvw_got.wait_recv()
     project(1)
-    ctx_got1 = attend_forward(1)
+    ctx_got = {}
+    for c in range(2):
+        ctx_got[1, c] = attend_forward(1, c)
+    ctx_got[1, 0].wait_recv()
+    reduce_send(0, 0, out_rows(1, 0))
     hid_got[0].wait_recv()
     project(0)
-    ctx_got1.wait_recv()
-    rs1 = [reduce_send(0, c, out_rows(1, c)) for c in range(2)]
-    ctx_got0 = attend_forward(0)
-    ctx_got0.wait_recv()
-    for c in range(2):
+    ctx_got[1, 1].wait_recv()
+    reduce_send(0, 1, out_rows(1, 1))
+    for c in range(2):
+        ctx_got[0, c] = attend_forward(0, c)
+    for c in range(2):
+        ctx_got[0, c].wait_recv()
         acc[pl.ds(c * PART, PART), :] = out_rows(0, c)
 
-    stats1 = []
-    for c in range(2):
-        rs1[c].wait_recv()
+    mixed = (mixed_own, mixed_o)
+    mixed_sent = []
+    for c in range(2):
+        rs_sent[0, c].wait_recv()
 
         def gather(i):
             rows = span(c * PART + i * STEP, STEP, 64)
@@ -411,11 +404,7 @@
             stat_send[0, rows, :] = stat_pack([row_sum(r), row_sum(r * r)])
 
         tiles(PART // STEP, gather)
-        stats1.append(stat_exchange(0, c))
-    mixed = (mixed_own, mixed_o)
-    mixed_sent = []
-    for c in range(2):
-        stats1[c].wait_recv()
+        stat_exchange(0, c).wait_recv()
 
         def normalize(i):
             rows = span(c * PART + i * STEP, STEP, 64)
@@ -448,31 +437,37 @@
         tiles(PART // 32, bend)
         return net.send(act_own.at[s, here], act_o.at[s, here], twin)
 
+    def contract_rows(s, c):
+        here = pl.ds(c * PART, PART)
+        return mm(act_own[s, here, :], dn_w[span(n * 1024, 1024), :]) + mm(
+            act_o[s, here, :], dn_w[span((1 - n) * 1024, 1024), :]
+        )
+
     act_got = {}
+    passed = []
     for c in range(2):
         mixed_sent[c][1].wait_recv()
         act_got[0, c] = expand(0, c)
-    for c in range(2):
-        pass_on(mixed, c, mixed_sent[c][0]).wait_recv()
-        act_got[1, c] = expand(1, c)
-
-    def contract_rows(s, c):
-        here = pl.ds(c * PART, PART)
-        return mm(act_own[s, here, :], dn_w[span(n * 1024, 1024), :]) + mm(
-            act_o[s, here, :], dn_w[span((1 - n) * 1024, 1024), :]
-        )
-
-    rs2 = []
-    for c in range(2):
-        act_got[1, c].wait_recv()
-        rs2.append(reduce_send(1, c, contract_rows(1, c)))
-    for c in range(2):
-        act_got[0, c].wait_recv()
-        acc[pl.ds(c * PART, PART), :] = contract_rows(0, c)
-
-    stats2 = []
-    for c in range(2):
-        rs2[c].wait_recv()
+        if c == 0:
+            passed.append(pass_on(mixed, 0, mixed_sent[0][0]))
+    passed[0].wait_recv()
+    act_got[1, 0] = expand(1, 0)
+    passed.append(pass_on(mixed, 1, mixed_sent[1][0]))
+    act_got[0, 0].wait_recv()
+    acc[pl.ds(0, PART), :] = contract_rows(0, 0)
+    act_got[1, 0].wait_recv()
+    reduce_send(1, 0, contract_rows(1, 0))
+    passed[1].wait_recv()
+    act_got[1, 1] = expand(1, 1)
+    act_got[0, 1].wait_recv()
+    acc[pl.ds(PART, PART), :] = contract_rows(0, 1)
+    act_got[1, 1].wait_recv()
+    reduce_send(1, 1, contract_rows(1, 1))
+
+    grad_down = (gd_own, gd_o)
+    gd_sent = []
+    for c in range(2):
+        rs_sent[1, c].wait_recv()
 
         def gather(i):
             rows = span(c * PART + i * STEP, STEP, 64)
@@ -485,11 +480,7 @@
             )
 
         tiles(PART // STEP, gather)
-        stats2.append(stat_exchange(1, c))
-    grad_down = (gd_own, gd_o)
-    gd_sent = []
-    for c in range(2):
-        stats2[c].wait_recv()
+        stat_exchange(1, c).wait_recv()
 
         def normalize(i):
             rows = span(c * PART + i * STEP, STEP, 64)
@@ -526,27 +517,32 @@
         tiles(PART // 32, bend)
         return net.send(gu_own.at[s, here], gu_o.at[s, here], twin)
 
+    def mixed_back(s, c):
+        here = pl.ds(c * PART, PART)
+        return mm_right(gu_own[s, here, :], up_w[:, span(n * 1024, 1024)]) + mm_right(
+            gu_o[s, here, :], up_w[:, span((1 - n) * 1024, 1024)]
+        )
+
     gu_got = {}
+    passed = []
     for c in range(2):
         gd_sent[c][1].wait_recv()
         gu_got[0, c] = shrink_back(0, c)
-    for c in range(2):
-        pass_on(grad_down, c, gd_sent[c][0]).wait_recv()
-        gu_got[1, c] = shrink_back(1, c)
-
-    def mixed_back(s, c):
-        here = pl.ds(c * PART, PART)
-        return mm_right(gu_own[s, here, :], up_w[:, span(n * 1024, 1024)]) + mm_right(
-            gu_o[s, here, :], up_w[:, span((1 - n) * 1024, 1024)]
-        )
-
-    rs3 = []
-    for c in range(2):
-        gu_got[1, c].wait_recv()
-        rs3.append(reduce_send(2, c, mixed_back(1, c)))
-    for c in range(2):
-        gu_got[0, c].wait_recv()
-        acc[pl.ds(c * PART, PART), :] = mixed_back(0, c)
+        if c == 0:
+            passed.append(pass_on(grad_down, 0, gd_sent[0][0]))
+    passed[0].wait_recv()
+    gu_got[1, 0] = shrink_back(1, 0)
+    passed.append(pass_on(grad_down, 1, gd_sent[1][0]))
+    gu_got[0, 0].wait_recv()
+    acc[pl.ds(0, PART), :] = mixed_back(0, 0)
+    gu_got[1, 0].wait_recv()
+    reduce_send(2, 0, mixed_back(1, 0))
+    passed[1].wait_recv()
+    gu_got[1, 1] = shrink_back(1, 1)
+    gu_got[0, 1].wait_recv()
+    acc[pl.ds(PART, PART), :] = mixed_back(0, 1)
+    gu_got[1, 1].wait_recv()
+    reduce_send(2, 1, mixed_back(1, 1))
 
     def feed_forward_grads():
         for part, (a, g) in enumerate(((act_own, gu_own), (act_o, gu_o))):
@@ -581,14 +577,21 @@
             column_add(SMALL_DOWN, gd_own[s].astype(F32))
 
     feed_forward_grads()
-
-    stats3 = []
-    for c in range(2):
-        rs3[c].wait_recv()
+    sum1 = Summing(
+        packed,
+        lambda q, place, size: landing1.at[q, pl.ds(place, size), :],
+        fin, out, (ss1, rs1_sem, ls1), 0, UP_ROWS + DOWN_ROWS, 0, table,
+    )
+    sum1.open()
+
+    grad_attn = (ga_own, ga_o)
+    ga_sent = []
+    for c in range(2):
+        rs_sent[2, c].wait_recv()
 
         def gather(i):
             rows = span(c * PART + i * STEP, STEP, 64)
-            g = res2[rows, :] + acc[rows, :] + rs_recv[2, rows, :].astype(F32)
+            g = res2[rows, :] + acc[rows, :] + rs_recv[0, rows, :].astype(F32)
             res2[rows, :] = g
             e = g * gain1[...]
             n1 = res1[rows, :]
@@ -597,11 +600,7 @@
             column_add(SMALL_NORM + 2, g)
 
         tiles(PART // STEP, gather)
-        stats3.append(stat_exchange(2, c))
-    grad_attn = (ga_own, ga_o)
-    ga_sent = []
-    for c in range(2):
-        stats3[c].wait_recv()
+        stat_exchange(2, c).wait_recv()
 
         def normalize(i):
             rows = span(c * PART + i * STEP, STEP, 64)
@@ -640,20 +639,23 @@
             dqs = jnp.where(low, dq[0], dq[1]) * scale
             dks = pltpu.roll(jnp.where(low, dk[0], dk[1]) * scale, 64, 1)
             dvs = jnp.where(low, dv[0], dv[1])
-            dqkv_own[s, :, span(p * 384, 128)] = jnp.where(low, dqs, dks).astype(BF)
-            dqkv_own[s, :, span(p * 384 + 128, 128)] = jnp.where(low, dvs, dqs).astype(BF)
-            dqkv_own[s, :, span(p * 384 + 256, 128)] = jnp.where(low, dks, dvs).astype(BF)
+            act_own[s, :, span(p * 384, 128)] = jnp.where(low, dqs, dks).astype(BF)
+            act_own[s, :, span(p * 384 + 128, 128)] = jnp.where(low, dvs, dqs).astype(BF)
+            act_own[s, :, span(p * 384 + 256, 128)] = jnp.where(low, dks, dvs).astype(BF)
 
         tiles(2, block)
-        return net.send(dqkv_own.at[s], dqkv_o.at[s], twin)
-
+        return net.send(act_own.at[s, :, pl.ds(0, 768)], slope.at[s, :, pl.ds(0, 768)], twin)
+
+    net.drain(act_got.values())
     for c in range(2):
         ga_sent[c][1].wait_recv()
     dqkv_got = [attend_back(0), None]
-    ga_passed = [pass_on(grad_attn, c, ga_sent[c][0]) for c in range(2)]
-    for copy in ga_passed:
+    passed = [pass_on(grad_attn, c, ga_sent[c][0]) for c in range(2)]
+    sum1.advance(0)
+    for copy in passed:
         copy.wait_recv()
     dqkv_got[1] = attend_back(1)
+    sum1.advance(1)
 
     for part, ctx in enumerate((ctx_own, ctx_o)):
         side = n if part == 0 else 1 - n
@@ -661,20 +663,9 @@
         packed[span(OUT_BASE + side * 256, 256), :] = got.astype(BF)
     for s in range(2):
         column_add(SMALL_OUT, ga_own[s].astype(F32))
-
-    def input_rows(s, c):
-        here = pl.ds(c * PART, PART)
-        return mm_right(dqkv_own[s, here, :], qkv_w[:, span(n * 768, 768)]) + mm_right(
-            dqkv_o[s, here, :], qkv_w[:, span((1 - n) * 768, 768)]
-        )
-
+    dqkv_got[0].wait_recv()
     dqkv_got[1].wait_recv()
-    rs4 = [reduce_send(3, c, input_rows(1, c)) for c in range(2)]
-    dqkv_got[0].wait_recv()
-    for c in range(2):
-        acc[pl.ds(c * PART, PART), :] = input_rows(0, c)
-
-    for part, g in enumerate((dqkv_own, dqkv_o)):
+    for part, g in enumerate((act_own, slope)):
         side = n if part == 0 else 1 - n
 
         def qkv_block(i):
@@ -698,16 +689,49 @@
             small[pl.ds(SMALL_QKV + side * 3 + j, 1), :] = total
 
         tiles(3, qkv_bias)
-
-    for c in range(2):
-        rs4[c].wait_recv()
+    sum2 = Summing(
+        packed,
+        lambda q, place, size: act_o.at[q // 2, pl.ds(place, size), pl.ds((q % 2) * 512, 512)],
+        fin, out, (ss2, rs2_sem, ls2), UP_ROWS + DOWN_ROWS, QKV_ROWS + OUT_ROWS, 256, table,
+    )
+    sum2.open()
+    smalls = SmallSum(small, small_kept, small_recv, (small_ss, small_rs), table)
+    smalls.begin(0)
+
+    def input_rows(s, c):
+        here = pl.ds(c * PART, PART)
+        return mm_right(act_own[s, here, 0:768], qkv_w[:, span(n * 768, 768)]) + mm_right(
+            slope[s, here, 0:768], qkv_w[:, span((1 - n) * 768, 768)]
+        )
+
+    for c in range(2):
+        reduce_send(3, c, input_rows(1, c))
+    sum1.advance(2)
+    for c in range(2):
+        acc[pl.ds(c * PART, PART), :] = input_rows(0, c)
+    sum1.advance(3)
+    sum2.advance(0)
+    smalls.take(0)
+    sum1.advance(4)
+    sum2.advance(1)
+    smalls.take(1)
+    sum1.advance(5)
+    for c in range(2):
+        rs_sent[3, c].wait_recv()
 
         def finish(i):
             rows = span(c * PART + i * STEP, STEP, 64)
-            in_grad[rows, :] = res2[rows, :] + acc[rows, :] + rs_recv[3, rows, :].astype(F32)
+            in_grad[rows, :] = res2[rows, :] + acc[rows, :] + rs_recv[1, rows, :].astype(F32)
 
         tiles(PART // STEP, finish)
-    net.close()
+    for step in range(2, 9):
+        sum2.advance(step)
+        if step < 6:
+            smalls.take(step)
+        if step + 4 < 9:
+            sum1.advance(step + 4)
+    for work in (net, sum1, sum2, smalls):
+        work.close()
 
 
 def layer_call(*arrays):
@@ -716,12 +740,13 @@
         ((2, SEQ, 512), BF), ((512, 768), BF), ((256, 512), BF), ((512, 1024), BF), ((1024, 512), BF),
         ((2, 2, SEQ, 128), BF), ((2, 2, SEQ, 128), BF), ((2, 2, SEQ, 128), BF),
         ((2, 4, SEQ, SEQ), BF), ((2, SEQ, 256), BF), ((2, SEQ, 256), BF),
-        ((4, SEQ, 512), BF), ((4, SEQ, 512), BF), ((3, SEQ, 128), F32), ((3, SEQ, 128), F32),
+        ((2, SEQ, 512), BF), ((2, SEQ, 512), BF), ((3, SEQ, 128), F32), ((3, SEQ, 128), F32),
         ((SEQ, 512), F32), ((SEQ, 512), F32), ((SEQ, 512), F32), ((SEQ, 128), F32), ((PART, 1024), F32),
         ((2, SEQ, 512), BF), ((2, SEQ, 512), BF), ((2, SEQ, 1024), BF), ((2, SEQ, 1024), BF),
         ((2, SEQ, 1024), BF), ((2, SEQ, 512), BF), ((2, SEQ, 512), BF), ((2, SEQ, 1024), BF),
         ((2, SEQ, 1024), BF), ((2, SEQ, 512), BF), ((2, SEQ, 512), BF),
-        ((SEQ, 256), BF), ((2, SEQ, 768), BF), ((2, SEQ, 768), BF),
+        ((SEQ, 256), BF), ((PACKED_ROWS, PACK), BF), ((4, 1024, PACK), BF), ((384, PACK), BF),
+        ((6, ROWS_SMALL, 256), F32), ((6, ROWS_SMALL, 256), F32),
     ]
     return pl.pallas_call(
         layer_kernel,
@@ -732,9 +757,14 @@
             jax.ShapeDtypeStruct((ROWS_SMALL, 256), F32),
         ),
         in_specs=[vmem] * len(arrays),
-        out_specs=(vmem,) * 4,
+        out_specs=(vmem, vmem, pl.BlockSpec(memory_space=pl.ANY), vmem),
         scratch_shapes=[pltpu.VMEM(*shape) for shape in shapes]
-        + [pltpu.SemaphoreType.DMA((MESSAGES,)), pltpu.SemaphoreType.DMA((MESSAGES,))],
+        + [
+            pltpu.SemaphoreType.DMA(shape)
+            for shape in (
+                (MESSAGES,), (MESSAGES,), (4, 9), (4, 9), (4,), (4, 9), (4, 9), (4,), (6,), (6,)
+            )
+        ],
         compiler_params=pltpu.CompilerParams(
             collective_id=2, has_side_effects=True, vmem_limit_bytes=60 * 2**20
         ),
@@ -760,12 +790,11 @@
 ):
     half_width = hidden_in.shape[1]
     heads_here, head_width = qkv_weight.shape[1], qkv_weight.shape[3]
-    hidden_out, input_grad, packed, small = layer_call(
+    hidden_out, input_grad, total, small = layer_call(
         hidden_in,
-        segment_ids.reshape(2, SEQ),
-        segment_ids.reshape(-1, 1),
+        segment_ids.reshape(-1, 128),
         qkv_weight.reshape(half_width, -1),
-        qv_bias.reshape(heads_here, -1),
+        qv_bias,
         out_weight.reshape(-1, half_width),
         out_bias[None],
         norm1_gain[None],
@@ -778,12 +807,10 @@
         norm2_shift[None],
         out_grad,
     )
-    total, small = sum_over_dp(packed, small)
-    total = total.astype(F32)
 
     def columns(base, rows):
         return jnp.concatenate(
-            [total[i : i + half_width] for i in range(base, base + rows, half_width)], 1
+            [total[i : i + half_width].astype(F32) for i in range(base, base + rows, half_width)], 1
         )
 
     qkv_sums = small[SMALL_QKV : SMALL_QKV + 6].reshape(heads_here, 3, head_width)
@@ -793,13 +820,13 @@
         input_grad,
         columns(QKV_BASE, QKV_ROWS).reshape(half_width, heads_here, 3, head_width),
         jnp.stack([qkv_sums[:, 0], qkv_sums[:, 2]], 1),
-        total[OUT_BASE : OUT_BASE + OUT_ROWS].reshape(heads_here, head_width, half_width),
+        total[OUT_BASE : OUT_BASE + OUT_ROWS].astype(F32).reshape(heads_here, head_width, half_width),
         small[SMALL_OUT : SMALL_OUT + 2].reshape(-1),
         norms[0],
         norms[1],
         columns(UP_BASE, UP_ROWS),
         small[SMALL_UP : SMALL_UP + 8].reshape(-1),
-        total[DOWN_BASE : DOWN_BASE + DOWN_ROWS],
+        total[DOWN_BASE : DOWN_BASE + DOWN_ROWS].astype(F32),
         small[SMALL_DOWN : SMALL_DOWN + 2].reshape(-1),
         norms[2],
         norms[3],

time: 254 us -> 206 us (0.81)
  Pallas kernels: 223 us -> 180 us
  local copies, waits for them, and re-layouts: 26.3 us -> 15.8 us
  other arithmetic: 3.2 us -> 9.01 us
    pallas_call x1 -> x0, Pallas kernels: 92.4 us -> none  [sum_over_dp(): pl.pallas_call(sum_kernel, out_shape=(jax.ShapeDtypeStruct((rows, PACK),...]
    pallas_call x1, Pallas kernels: 130 us -> 180 us  [layer_call(): pl.pallas_call(layer_kernel, out_shape=(jax.ShapeDtypeStruct((SEQ, 512),...]
    slice x2 -> x1, local copies, waits for them, and re-layouts: 6.48 us -> 0.27 us  [columns(): total[i:i + half_width].astype(F32)]
    convert_element_type x0 -> x1, other arithmetic: none -> 4.35 us  [per_device(): total[DOWN_BASE:DOWN_BASE + DOWN_ROWS].astype(F32)]
where the time goes in v3:
time: 206 us
  Pallas kernels  180 us (87%)
  local copies, waits for them, and re-layouts  15.8 us (8%)
  other arithmetic  9.01 us (4%)
    pallas_call x1, Pallas kernels, layer_call(): pl.pallas_call(layer_kernel, out_shape=(jax.ShapeDtypeStruct((SEQ, 512),...  180 us
    unnamed x13, local copies, waits for them, and re-layouts  9.78 us
    convert_element_type x1, other arithmetic, per_device(): total[DOWN_BASE:DOWN_BASE + DOWN_ROWS].astype(F32)  4.35 us

profile of v3, /device:TPU:0, one launch (start us, length us, event | category | flops | bytes accessed | tf_op | source)
XLA Modules:
  0.0 205.7 jit_solution(991629425933192595)
XLA Ops:
  0.6 2.6 %copy.31.qkv_w = bf16[512,1536]{1,0:T(8,128)(2,1)} copy(bf16[512,1536]{0,1:T(8,128)(2,1)} %bitcast.36) | data formatting | bytes 3145728 | tf_op jit(solution)/shard_map/reshape | solution.py:796
  3.2 180.2 %shard_map.254 = (bf16[512,512]{1,0:T(8,128)(2,1)}, f32[512,512]{1,0:T(8,128)}, bf16[6144,512]{1,0:T(8,128)(2,1)}, f32[32,256]{1,0:T(8,128)}) custom-call(bf16[1024,512]{1,0:T(8,128)(2,1)} %hid.1, s32[8,128]{1,0:T(8,128)} %bitcast.40, bf16[512,1536]{1,0:T(8,128)(2,1)} %copy.31.qkv_w, f32[8,2,64]{2,1,0:T(2,128)} %qv_b.1, bf16[512,512]{1,0:T(8,128)(2,1)} %bitcast.37, ...), custom_call_target="tpu_custom_call" | custom-call | tf_op jit(solution)/shard_map/pallas_call | solution.py:751
  183.4 0.7 slice_bitcast_fusion
  184.1 0.6 copy.36
  184.7 0.7 slice.69
  185.4 0.9 slice_bitcast_fusion.1
  186.3 0.6 copy.39
  186.9 0.6 copy.38
  187.4 0.6 copy.37
  188.0 0.6 copy.35
  188.6 0.6 copy.34
  189.2 0.6 copy.33
  189.8 0.1 reshape.75
  189.9 0.6 pad_maximum_fusion
  190.5 0.0 copy-start
  190.5 4.3 %slice_convert_fusion = f32[2048,512]{1,0:T(8,128)} fusion(bf16[6144,512]{1,0:T(8,128)(2,1)} %get-tuple-element.20), kind=kLoop, calls=%fused_computation.1 | loop fusion | flops 1048576 | bytes 6291456 | tf_op jit(solution)/shard_map/convert_element_type | solution.py:829
  194.8 0.0 copy-done
  194.8 0.3 fusion
  195.1 1.1 convert.4
  196.2 2.6 %maximum_convert_fusion = f32[512,2048]{1,0:T(8,128)} fusion(bf16[512,512]{1,0:T(8,128)(2,1)S(1)} %get-tuple-element.37, bf16[512,512]{1,0:T(8,128)(2,1)S(1)} %get-tuple-element.38, bf16[512,512]{1,0:T(8,128)(2,1)S(1)} %get-tuple-element.39, bf16[512,512]{1,0:T(8,128)(2,1)S(1)} %get-tuple-element.36), kind=kLoop, calls=%fused_computation | loop fusion | flops 8388608 | bytes 6291456 | tf_op jit(solution)/shard_map/concatenate | solution.py:812
  198.8 0.4 maximum_convert_fusion.1
  199.2 2.4 %copy.32 = f32[512,1536]{0,1:T(8,128)} copy(f32[512,1536]{1,0:T(8,128)S(1)} %maximum_convert_fusion.1) | data formatting | bytes 6291456 | tf_op jit(solution)/shard_map/reshape | solution.py:821
  201.5 1.9 copy.42
  203.4 2.3 %copy.43 = f32[512,512]{1,0:T(8,128)} copy(f32[512,512]{1,0:T(8,128)} %get-tuple-element.67) | data formatting | bytes 2097152
  (1 shorter events, 0.0 us)
Async XLA Ops:
  190.5 4.4 %copy-start = (bf16[6144,512]{1,0:T(8,128)(2,1)S(1)}, bf16[6144,512]{1,0:T(8,128)(2,1)}, u32[]{:S(2)}) copy-start(bf16[6144,512]{1,0:T(8,128)(2,1)} %get-tuple-element.20) | copy-start | bytes 18874372

commit v4 on v3

--- a/solution.py
+++ b/solution.py
@@ -44,8 +44,8 @@
 
 
 class Summing:
-    def __init__(self, buf, landing, fin, out, sems, base, rows, fin_base, table):
-        self.buf, self.landing, self.fin, self.out = buf, landing, fin, out
+    def __init__(self, buf, landing, fin, out_at, sems, base, rows, fin_base, table):
+        self.buf, self.landing, self.fin, self.out_at = buf, landing, fin, out_at
         self.send_sem, self.recv_sem, self.local_sem = sems
         self.table, self.fin_base = table, fin_base
         self.quarter = rows // 4
@@ -83,7 +83,7 @@
         else:
             level = 9 - step
             name, size = ORDERS[q][level - 1], self.size(level)
-            dst = self.out.at[pl.ds(self.offsets[q][level], size), :]
+            dst = self.out_at(q, self.offsets[q][level], size)
             src = self.fin.at[self.final(q), :] if step == 5 else dst
         return pltpu.make_async_remote_copy(
             src_ref=src,
@@ -95,10 +95,8 @@
         )
 
     def keep(self, q):
-        where = pl.ds(self.offsets[q][4], self.size(4))
-        return pltpu.make_async_copy(
-            self.fin.at[self.final(q), :], self.out.at[where, :], self.local_sem.at[q]
-        )
+        where = self.out_at(q, self.offsets[q][4], self.size(4))
+        return pltpu.make_async_copy(self.fin.at[self.final(q), :], where, self.local_sem.at[q])
 
     def begin(self, q, step):
         copy = self.make(q, step)
@@ -177,7 +175,9 @@
 
 
 SEQ = 512
-PART = 256
+PART = 128
+CHUNKS = SEQ // PART
+HALF = 256
 ROWS_SMALL = 32
 SMALL_QKV, SMALL_UP, SMALL_OUT, SMALL_DOWN, SMALL_NORM = 0, 6, 14, 16, 24
 HALF_ROOT = 0.7071067811865476
@@ -236,13 +236,14 @@
         self.drain(self.sent)
 
 
-MESSAGES = 64
+MESSAGES = 96
 
 
 def layer_kernel(
-    hid, seg, qkv_w, qv_b, out_w, out_b, gain1, shift1, up_w, up_b, dn_w, dn_b,
-    gain2, shift2, dy,
-    hid_out, in_grad, out, small,
+    hid, seg, qkv_w, qv_b, out_src, out_b, gain1, shift1, up_src, up_b, dn_src, dn_b,
+    gain2, shift2, dy_src,
+    hid_out, in_grad, sum_qkv, sum_out, sum_up, sum_down, small,
+    out_w, up_w, dn_w, dy, load_sem,
     hid_o, qkvw_o, outw_o, upw_o, dnw_o,
     qs, ks, vs, probs, ctx_own, ctx_o,
     rs_send, rs_recv, stat_send, stat_recv,
@@ -254,6 +255,12 @@
     dp, w, n = lax.axis_index("dp"), lax.axis_index("wide"), lax.axis_index("narrow")
     twin, peer = (dp, w, 1 - n), (dp, 1 - w, n)
     table = partner_table()
+    loads = [
+        pltpu.make_async_copy(src, dst, load_sem.at[i])
+        for i, (src, dst) in enumerate(((out_src, out_w), (up_src, up_w), (dn_src, dn_w), (dy_src, dy)))
+    ]
+    for load in loads:
+        load.start()
     barrier = pltpu.get_barrier_semaphore()
     for device in [twin] + [entry[0] for entry in table.values()]:
         pl.semaphore_signal(barrier, inc=1, device_id=device, device_id_type=MESH)
@@ -270,20 +277,18 @@
 
     hid_got = [None, None]
     hid_got[1] = net.send(hid.at[span(base_of[1], SEQ)], hid_o.at[1], twin)
-    qkvw_got = net.send(qkv_w.at[:, span((1 - n) * 768, 768)], qkvw_o, twin)
+    qkvw_got = net.send(qkv_w.at[span((1 - n) * 768, 768), :], qkvw_o, twin)
     hid_got[0] = net.send(hid.at[span(base_of[0], SEQ)], hid_o.at[0], twin)
-    upw_got = net.send(up_w.at[:, span((1 - n) * 1024, 1024)], upw_o, twin)
-    dnw_got = net.send(dn_w.at[span((1 - n) * 1024, 1024), :], dnw_o, twin)
-    outw_got = net.send(out_w.at[span((1 - n) * 256, 256), :], outw_o, twin)
 
     small[...] = jnp.zeros_like(small)
 
     def project(s):
         def block(i):
             p, r = i // 2, i % 2
-            here = span(r * PART, PART)
-            got = mm(hid[span(base_of[s] + r * PART, PART), :], qkv_w[:, span(n * 768 + p * 384, 384)])
-            got += mm(hid_o[s, here, :], qkvw_o[:, span(p * 384, 384)])
+            here = span(r * HALF, HALF)
+            mine = hid[span(base_of[s] + r * HALF, HALF), :]
+            got = mm_right(mine, qkv_w[span(n * 768 + p * 384, 384), :])
+            got += mm_right(hid_o[s, here, :], qkvw_o[span(p * 384, 384), :])
             b0, b1, b2 = got[:, :128], got[:, 128:256], got[:, 256:]
             head = n * 4 + 2 * p
             q_bias, v_bias = [
@@ -302,9 +307,9 @@
         return row, jnp.transpose(jnp.broadcast_to(row, (128, SEQ)))
 
     def attend_forward(s, r):
-        here = pl.ds(r * PART, PART)
+        here = pl.ds(r * HALF, HALF)
         row, column = segments(s)
-        same = column[r * PART : (r + 1) * PART, 0:1] == row
+        same = column[r * HALF : (r + 1) * HALF, 0:1] == row
 
         def block(p):
             q, k, v = qs[s, p, here, :], ks[s, p], vs[s, p]
@@ -328,6 +333,41 @@
 
     rs_sent = {}
 
+    def two_way(pair, sent, first, second, k):
+        passed, got = {}, {}
+
+        def own(c):
+            sent[c][1].wait_recv()
+            got[0, c] = first(0, c)
+
+        def hop(c):
+            passed[c] = pass_on(pair, c, sent[c][0])
+
+        def other(c):
+            passed[c].wait_recv()
+            got[1, c] = first(1, c)
+
+        def push(c):
+            got[1, c].wait_recv()
+            reduce_send(k, c, second(1, c))
+
+        own(0)
+        for c in range(CHUNKS):
+            if c + 1 < CHUNKS:
+                own(c + 1)
+            hop(c)
+            if c >= 1:
+                other(c - 1)
+            if c >= 2:
+                push(c - 2)
+        other(CHUNKS - 1)
+        push(CHUNKS - 2)
+        push(CHUNKS - 1)
+        for c in range(CHUNKS):
+            got[0, c].wait_recv()
+            acc[pl.ds(c * PART, PART), :] = second(0, c)
+        return got
+
     def reduce_send(k, c, rows):
         here = pl.ds(c * PART, PART)
         slot = k % 2
@@ -379,21 +419,26 @@
     ctx_got = {}
     for c in range(2):
         ctx_got[1, c] = attend_forward(1, c)
+    upw_got = net.send(up_src.at[:, span((1 - n) * 1024, 1024)], upw_o, twin)
+    loads[0].wait()
     ctx_got[1, 0].wait_recv()
-    reduce_send(0, 0, out_rows(1, 0))
+    for c in range(CHUNKS // 2):
+        reduce_send(0, c, out_rows(1, c))
     hid_got[0].wait_recv()
     project(0)
     ctx_got[1, 1].wait_recv()
-    reduce_send(0, 1, out_rows(1, 1))
+    for c in range(CHUNKS // 2, CHUNKS):
+        reduce_send(0, c, out_rows(1, c))
     for c in range(2):
         ctx_got[0, c] = attend_forward(0, c)
-    for c in range(2):
-        ctx_got[0, c].wait_recv()
-        acc[pl.ds(c * PART, PART), :] = out_rows(0, c)
+    for half in range(2):
+        ctx_got[0, half].wait_recv()
+        for c in range(half * CHUNKS // 2, (half + 1) * CHUNKS // 2):
+            acc[pl.ds(c * PART, PART), :] = out_rows(0, c)
 
     mixed = (mixed_own, mixed_o)
     mixed_sent = []
-    for c in range(2):
+    for c in range(CHUNKS):
         rs_sent[0, c].wait_recv()
 
         def gather(i):
@@ -418,6 +463,8 @@
         tiles(PART // STEP, normalize)
         mixed_sent.append(spread(mixed, c))
 
+    dnw_got = net.send(dn_src.at[span((1 - n) * 1024, 1024), :], dnw_o, twin)
+    loads[1].wait()
     upw_got.wait_recv()
 
     def expand(s, c):
@@ -443,30 +490,14 @@
             act_o[s, here, :], dn_w[span((1 - n) * 1024, 1024), :]
         )
 
-    act_got = {}
-    passed = []
-    for c in range(2):
-        mixed_sent[c][1].wait_recv()
-        act_got[0, c] = expand(0, c)
-        if c == 0:
-            passed.append(pass_on(mixed, 0, mixed_sent[0][0]))
-    passed[0].wait_recv()
-    act_got[1, 0] = expand(1, 0)
-    passed.append(pass_on(mixed, 1, mixed_sent[1][0]))
-    act_got[0, 0].wait_recv()
-    acc[pl.ds(0, PART), :] = contract_rows(0, 0)
-    act_got[1, 0].wait_recv()
-    reduce_send(1, 0, contract_rows(1, 0))
-    passed[1].wait_recv()
-    act_got[1, 1] = expand(1, 1)
-    act_got[0, 1].wait_recv()
-    acc[pl.ds(PART, PART), :] = contract_rows(0, 1)
-    act_got[1, 1].wait_recv()
-    reduce_send(1, 1, contract_rows(1, 1))
-
+    loads[2].wait()
+    act_got = two_way(mixed, mixed_sent, expand, contract_rows, 1)
+
+    outw_got = net.send(out_src.at[span((1 - n) * 256, 256), :], outw_o, twin)
+    loads[3].wait()
     grad_down = (gd_own, gd_o)
     gd_sent = []
-    for c in range(2):
+    for c in range(CHUNKS):
         rs_sent[1, c].wait_recv()
 
         def gather(i):
@@ -523,26 +554,7 @@
             gu_o[s, here, :], up_w[:, span((1 - n) * 1024, 1024)]
         )
 
-    gu_got = {}
-    passed = []
-    for c in range(2):
-        gd_sent[c][1].wait_recv()
-        gu_got[0, c] = shrink_back(0, c)
-        if c == 0:
-            passed.append(pass_on(grad_down, 0, gd_sent[0][0]))
-    passed[0].wait_recv()
-    gu_got[1, 0] = shrink_back(1, 0)
-    passed.append(pass_on(grad_down, 1, gd_sent[1][0]))
-    gu_got[0, 0].wait_recv()
-    acc[pl.ds(0, PART), :] = mixed_back(0, 0)
-    gu_got[1, 0].wait_recv()
-    reduce_send(2, 0, mixed_back(1, 0))
-    passed[1].wait_recv()
-    gu_got[1, 1] = shrink_back(1, 1)
-    gu_got[0, 1].wait_recv()
-    acc[pl.ds(PART, PART), :] = mixed_back(0, 1)
-    gu_got[1, 1].wait_recv()
-    reduce_send(2, 1, mixed_back(1, 1))
+    two_way(grad_down, gd_sent, shrink_back, mixed_back, 2)
 
     def feed_forward_grads():
         for part, (a, g) in enumerate(((act_own, gu_own), (act_o, gu_o))):
@@ -577,16 +589,29 @@
             column_add(SMALL_DOWN, gd_own[s].astype(F32))
 
     feed_forward_grads()
+
+    def feed_forward_out(q, start, size):
+        if q < 2:
+            return sum_up.at[
+                pl.ds(pl.multiple_of(start % 512, 16), size), span(start // 512 * 512, 512)
+            ]
+        return sum_down.at[pl.ds(pl.multiple_of(start - DOWN_BASE, 16), size), :]
+
+    def attention_out(q, start, size):
+        if q < 3:
+            return sum_qkv.at[pl.ds(pl.multiple_of(start - QKV_BASE, 16), size), :]
+        return sum_out.at[pl.ds(pl.multiple_of(start - OUT_BASE, 16), size), :]
+
     sum1 = Summing(
         packed,
         lambda q, place, size: landing1.at[q, pl.ds(place, size), :],
-        fin, out, (ss1, rs1_sem, ls1), 0, UP_ROWS + DOWN_ROWS, 0, table,
+        fin, feed_forward_out, (ss1, rs1_sem, ls1), 0, UP_ROWS + DOWN_ROWS, 0, table,
     )
     sum1.open()
 
     grad_attn = (ga_own, ga_o)
     ga_sent = []
-    for c in range(2):
+    for c in range(CHUNKS):
         rs_sent[2, c].wait_recv()
 
         def gather(i):
@@ -619,43 +644,50 @@
 
     outw_got.wait_recv()
 
-    def attend_back(s):
+    def context_back(s):
         dctx[...] = (
             mm_right(ga_own[s], out_w[span(n * 256, 256), :]) + mm_right(ga_o[s], outw_o[...])
         ).astype(BF)
 
-        def block(p):
-            q, k, v, d = qs[s, p], ks[s, p], vs[s, p], dctx[:, span(p * 128, 128)]
-            dq, dk, dv = [], [], []
-            for h in range(2):
-                weight = probs[s, p * 2 + h]
-                wide_weight = weight.astype(F32)
-                dprob = mm_right(d * picks[h], v)
-                inner = jnp.sum(dprob * wide_weight, -1, keepdims=True)
-                dscore = (wide_weight * (dprob - inner)).astype(BF)
-                dq.append(mm(dscore, k))
-                dk.append(mm_left(dscore, q))
-                dv.append(mm_left(weight, d))
-            dqs = jnp.where(low, dq[0], dq[1]) * scale
-            dks = pltpu.roll(jnp.where(low, dk[0], dk[1]) * scale, 64, 1)
-            dvs = jnp.where(low, dv[0], dv[1])
-            act_own[s, :, span(p * 384, 128)] = jnp.where(low, dqs, dks).astype(BF)
-            act_own[s, :, span(p * 384 + 128, 128)] = jnp.where(low, dvs, dqs).astype(BF)
-            act_own[s, :, span(p * 384 + 256, 128)] = jnp.where(low, dks, dvs).astype(BF)
-
-        tiles(2, block)
+    def back_pair(s, p):
+        q, k, v, d = qs[s, p], ks[s, p], vs[s, p], dctx[:, span(p * 128, 128)]
+        dq, dk, dv = [], [], []
+        for h in range(2):
+            weight = probs[s, p * 2 + h]
+            wide_weight = weight.astype(F32)
+            dprob = mm_right(d * picks[h], v)
+            inner = jnp.sum(dprob * wide_weight, -1, keepdims=True)
+            dscore = (wide_weight * (dprob - inner)).astype(BF)
+            dq.append(mm(dscore, k))
+            dk.append(mm_left(dscore, q))
+            dv.append(mm_left(weight, d))
+        dqs = jnp.where(low, dq[0], dq[1]) * scale
+        dks = pltpu.roll(jnp.where(low, dk[0], dk[1]) * scale, 64, 1)
+        dvs = jnp.where(low, dv[0], dv[1])
+        act_own[s, :, span(p * 384, 128)] = jnp.where(low, dqs, dks).astype(BF)
+        act_own[s, :, span(p * 384 + 128, 128)] = jnp.where(low, dvs, dqs).astype(BF)
+        act_own[s, :, span(p * 384 + 256, 128)] = jnp.where(low, dks, dvs).astype(BF)
+
+    def send_qkv(s):
         return net.send(act_own.at[s, :, pl.ds(0, 768)], slope.at[s, :, pl.ds(0, 768)], twin)
 
     net.drain(act_got.values())
-    for c in range(2):
+    for c in range(CHUNKS):
         ga_sent[c][1].wait_recv()
-    dqkv_got = [attend_back(0), None]
-    passed = [pass_on(grad_attn, c, ga_sent[c][0]) for c in range(2)]
     sum1.advance(0)
+    context_back(0)
+    back_pair(0, 0)
+    back_pair(0, 1)
+    dqkv_got = [send_qkv(0)]
+    passed = [pass_on(grad_attn, c, ga_sent[c][0]) for c in range(CHUNKS)]
+    sum1.advance(1)
     for copy in passed:
         copy.wait_recv()
-    dqkv_got[1] = attend_back(1)
-    sum1.advance(1)
+    context_back(1)
+    back_pair(1, 0)
+    back_pair(1, 1)
+    dqkv_got.append(send_qkv(1))
+    sum1.advance(2)
 
     for part, ctx in enumerate((ctx_own, ctx_o)):
         side = n if part == 0 else 1 - n
@@ -668,18 +700,14 @@
     for part, g in enumerate((act_own, slope)):
         side = n if part == 0 else 1 - n
 
-        def qkv_block(i):
-            j, r = i // 2, i % 2
-            cols, where = span(j * 256, 256), span(r * 256, 256)
-            got = mm_left(hid[span(base_of[0], SEQ), where], g[0, :, cols]) + mm_left(
-                hid[span(base_of[1], SEQ), where], g[1, :, cols]
+        def qkv_block(j):
+            cols = span(j * 256, 256)
+            got = mm_left(g[0, :, cols], hid[span(base_of[0], SEQ), :]) + mm_left(
+                g[1, :, cols], hid[span(base_of[1], SEQ), :]
             )
-            at = side * 3 + j
-            packed[
-                span(QKV_BASE + (at // 2) * 512 + r * 256, 256), span((at % 2) * 256, 256)
-            ] = got.astype(BF)
-
-        tiles(6, qkv_block)
+            packed[span(QKV_BASE + side * 768 + j * 256, 256), :] = got.astype(BF)
+
+        tiles(3, qkv_block)
 
         def qkv_bias(j):
             cols = span(j * 256, 256)
@@ -692,7 +720,7 @@
     sum2 = Summing(
         packed,
         lambda q, place, size: act_o.at[q // 2, pl.ds(place, size), pl.ds((q % 2) * 512, 512)],
-        fin, out, (ss2, rs2_sem, ls2), UP_ROWS + DOWN_ROWS, QKV_ROWS + OUT_ROWS, 256, table,
+        fin, attention_out, (ss2, rs2_sem, ls2), UP_ROWS + DOWN_ROWS, QKV_ROWS + OUT_ROWS, 256, table,
     )
     sum2.open()
     smalls = SmallSum(small, small_kept, small_recv, (small_ss, small_rs), table)
@@ -700,23 +728,24 @@
 
     def input_rows(s, c):
         here = pl.ds(c * PART, PART)
-        return mm_right(act_own[s, here, 0:768], qkv_w[:, span(n * 768, 768)]) + mm_right(
-            slope[s, here, 0:768], qkv_w[:, span((1 - n) * 768, 768)]
+        return mm(act_own[s, here, 0:768], qkv_w[span(n * 768, 768), :]) + mm(
+            slope[s, here, 0:768], qkv_w[span((1 - n) * 768, 768), :]
         )
 
-    for c in range(2):
+    sum1.advance(3)
+    for c in range(CHUNKS):
         reduce_send(3, c, input_rows(1, c))
-    sum1.advance(2)
-    for c in range(2):
+    for c in range(CHUNKS):
         acc[pl.ds(c * PART, PART), :] = input_rows(0, c)
-    sum1.advance(3)
+    smalls.take(0)
     sum2.advance(0)
-    smalls.take(0)
     sum1.advance(4)
+    smalls.take(1)
     sum2.advance(1)
-    smalls.take(1)
     sum1.advance(5)
-    for c in range(2):
+    sum2.advance(2)
+    smalls.take(2)
+    for c in range(CHUNKS):
         rs_sent[3, c].wait_recv()
 
         def finish(i):
@@ -724,20 +753,27 @@
             in_grad[rows, :] = res2[rows, :] + acc[rows, :] + rs_recv[1, rows, :].astype(F32)
 
         tiles(PART // STEP, finish)
-    for step in range(2, 9):
-        sum2.advance(step)
-        if step < 6:
-            smalls.take(step)
-        if step + 4 < 9:
-            sum1.advance(step + 4)
+    sum1.advance(6)
+    sum2.advance(3)
+    smalls.take(3)
+    sum2.advance(4)
+    smalls.take(4)
+    sum2.advance(5)
+    sum1.advance(7)
+    smalls.take(5)
+    sum2.advance(6)
+    sum2.advance(7)
+    sum1.advance(8)
+    sum2.advance(8)
     for work in (net, sum1, sum2, smalls):
         work.close()
 
 
 def layer_call(*arrays):
     vmem = pl.BlockSpec(memory_space=pltpu.VMEM)
+    anywhere = pl.BlockSpec(memory_space=pl.ANY)
     shapes = [
-        ((2, SEQ, 512), BF), ((512, 768), BF), ((256, 512), BF), ((512, 1024), BF), ((1024, 512), BF),
+        ((2, SEQ, 512), BF), ((768, 512), BF), ((256, 512), BF), ((512, 1024), BF), ((1024, 512), BF),
         ((2, 2, SEQ, 128), BF), ((2, 2, SEQ, 128), BF), ((2, 2, SEQ, 128), BF),
         ((2, 4, SEQ, SEQ), BF), ((2, SEQ, 256), BF), ((2, SEQ, 256), BF),
         ((2, SEQ, 512), BF), ((2, SEQ, 512), BF), ((3, SEQ, 128), F32), ((3, SEQ, 128), F32),
@@ -753,12 +789,22 @@
         out_shape=(
             jax.ShapeDtypeStruct((SEQ, 512), BF),
             jax.ShapeDtypeStruct((SEQ, 512), F32),
-            jax.ShapeDtypeStruct((PACKED_ROWS, PACK), BF),
+            jax.ShapeDtypeStruct((QKV_ROWS, PACK), BF),
+            jax.ShapeDtypeStruct((OUT_ROWS, PACK), BF),
+            jax.ShapeDtypeStruct((512, UP_ROWS), BF),
+            jax.ShapeDtypeStruct((DOWN_ROWS, PACK), BF),
             jax.ShapeDtypeStruct((ROWS_SMALL, 256), F32),
         ),
-        in_specs=[vmem] * len(arrays),
-        out_specs=(vmem, vmem, pl.BlockSpec(memory_space=pl.ANY), vmem),
-        scratch_shapes=[pltpu.VMEM(*shape) for shape in shapes]
+        in_specs=[anywhere if i in (4, 8, 10, 14) else vmem for i in range(len(arrays))],
+        out_specs=(vmem, vmem) + (anywhere,) * 4 + (vmem,),
+        scratch_shapes=[
+            pltpu.VMEM((512, 512), BF),
+            pltpu.VMEM((512, 2048), BF),
+            pltpu.VMEM((2048, 512), BF),
+            pltpu.VMEM((512, 512), BF),
+            pltpu.SemaphoreType.DMA((4,)),
+        ]
+        + [pltpu.VMEM(*shape) for shape in shapes]
         + [
             pltpu.SemaphoreType.DMA(shape)
             for shape in (
@@ -769,6 +815,62 @@
             collective_id=2, has_side_effects=True, vmem_limit_bytes=60 * 2**20
         ),
     )(*arrays)
+
+
+def finish_kernel(
+    hidden, grad, qkv, out, up, down, small,
+    hidden_o, grad_o, qkv_o, out_o, up_o, down_o, qvb_o, outb_o, upb_o, downb_o, g1_o, s1_o, g2_o, s2_o,
+):
+    hidden_o[...] = hidden[...]
+    grad_o[...] = grad[...]
+    qkv_o[...] = qkv[...].astype(F32)
+    out_o[...] = out[...].astype(F32)
+    up_o[...] = up[...].astype(F32)
+    down_o[...] = down[...].astype(F32)
+
+    @pl.when(pl.program_id(0) == 0)
+    def _():
+        for head in range(8):
+            for i in range(2):
+                row, lane = divmod(head * 192 + i * 128, 256)
+                row += SMALL_QKV
+                qvb_o[head, i : i + 1, :] = small[row : row + 1, lane : lane + 64]
+        bases = [SMALL_NORM + 2 * i for i in range(4)]
+        for ref, first, count in (
+            (outb_o, SMALL_OUT, 2),
+            (upb_o, SMALL_UP, 8),
+            (downb_o, SMALL_DOWN, 2),
+            (g1_o, bases[0], 2),
+            (s1_o, bases[1], 2),
+            (g2_o, bases[2], 2),
+            (s2_o, bases[3], 2),
+        ):
+            for j in range(count):
+                ref[:, j * 256 : (j + 1) * 256] = small[first + j : first + j + 1, :]
+
+
+def finish_call(hidden, grad, qkv, out, up, down, small):
+    steps = 8
+
+    def rows(shape):
+        return pl.BlockSpec((shape[0] // steps, shape[1]), lambda i: (i, 0))
+
+    def whole(shape):
+        return pl.BlockSpec(shape, lambda i: (0,) * len(shape))
+
+    big = [hidden, grad, qkv, out, up, down]
+    thin = [(8, 2, 64), (1, 512), (1, 2048), (1, 512)] + [(1, 512)] * 4
+    return pl.pallas_call(
+        finish_kernel,
+        grid=(steps,),
+        out_shape=[
+            jax.ShapeDtypeStruct(a.shape, BF if a is hidden else F32) for a in big
+        ]
+        + [jax.ShapeDtypeStruct(shape, F32) for shape in thin],
+        in_specs=[rows(a.shape) for a in big] + [whole(small.shape)],
+        out_specs=[rows(a.shape) for a in big] + [whole(shape) for shape in thin],
+        compiler_params=pltpu.CompilerParams(vmem_limit_bytes=60 * 2**20),
+    )(*big, small)
 
 
 def per_device(
@@ -790,10 +892,10 @@
 ):
     half_width = hidden_in.shape[1]
     heads_here, head_width = qkv_weight.shape[1], qkv_weight.shape[3]
-    hidden_out, input_grad, total, small = layer_call(
+    results = layer_call(
         hidden_in,
         segment_ids.reshape(-1, 128),
-        qkv_weight.reshape(half_width, -1),
+        qkv_weight.transpose(1, 2, 3, 0).reshape(-1, half_width),
         qv_bias,
         out_weight.reshape(-1, half_width),
         out_bias[None],
@@ -808,28 +910,22 @@
         out_grad,
     )
 
-    def columns(base, rows):
-        return jnp.concatenate(
-            [total[i : i + half_width].astype(F32) for i in range(base, base + rows, half_width)], 1
-        )
-
-    qkv_sums = small[SMALL_QKV : SMALL_QKV + 6].reshape(heads_here, 3, head_width)
-    norms = small[SMALL_NORM : SMALL_NORM + 8].reshape(4, half_width)
+    hidden_out, input_grad, qkv, out, up, down, qv, outb, upb, downb, *norms = finish_call(*results)
     return (
         hidden_out,
         input_grad,
-        columns(QKV_BASE, QKV_ROWS).reshape(half_width, heads_here, 3, head_width),
-        jnp.stack([qkv_sums[:, 0], qkv_sums[:, 2]], 1),
-        total[OUT_BASE : OUT_BASE + OUT_ROWS].astype(F32).reshape(heads_here, head_width, half_width),
-        small[SMALL_OUT : SMALL_OUT + 2].reshape(-1),
-        norms[0],
-        norms[1],
-        columns(UP_BASE, UP_ROWS),
-        small[SMALL_UP : SMALL_UP + 8].reshape(-1),
-        total[DOWN_BASE : DOWN_BASE + DOWN_ROWS].astype(F32),
-        small[SMALL_DOWN : SMALL_DOWN + 2].reshape(-1),
-        norms[2],
-        norms[3],
+        qkv.reshape(heads_here, 3, head_width, half_width).transpose(3, 0, 1, 2),
+        qv,
+        out.reshape(heads_here, head_width, half_width),
+        outb.reshape(-1),
+        norms[0].reshape(-1),
+        norms[1].reshape(-1),
+        up,
+        upb.reshape(-1),
+        down,
+        downb.reshape(-1),
+        norms[2].reshape(-1),
+        norms[3].reshape(-1),
     )
 
 

time: 206 us -> 184 us (0.89)
  local copies, waits for them, and re-layouts: 15.8 us -> 0 us
  other arithmetic: 9.01 us -> 0 us
    pallas_call x0 -> x1, Pallas kernels: none -> 9.82 us  [finish_call(): pl.pallas_call(finish_kernel, grid=(steps,), out_shape=[jax.ShapeDtypeStr...]
    unnamed x13 -> x0, local copies, waits for them, and re-layouts: 9.78 us -> none
    pallas_call x1, Pallas kernels: 180 us -> 173 us  [layer_call(): pl.pallas_call(layer_kernel, out_shape=(jax.ShapeDtypeStruct((SEQ, 512),...]
    reshape x3 -> x0, local copies, waits for them, and re-layouts: 5.03 us -> none  [the longest x1 2.58 us: per_device(): qkv_weight.reshape(half_width, -1)]
    convert_element_type x1 -> x0, other arithmetic: 4.35 us -> none  [per_device(): total[DOWN_BASE:DOWN_BASE + DOWN_ROWS].astype(F32)]
    concatenate x1 -> x0, other arithmetic: 2.56 us -> none  [columns(): jnp.concatenate([total[i:i + half_width].astype(F32) for i in range(base,...]
where the time goes in v4:
time: 184 us; the launch traced here: 183 us
  Pallas kernels  182 us (99%)
    pallas_call x1, Pallas kernels, layer_call(): pl.pallas_call(layer_kernel, out_shape=(jax.ShapeDtypeStruct((SEQ, 512),...  173 us
    pallas_call x1, Pallas kernels, finish_call(): pl.pallas_call(finish_kernel, grid=(steps,), out_shape=[jax.ShapeDtypeStr...  9.82 us

profile of v4, /device:TPU:0, one launch (start us, length us, event | category | flops | bytes accessed | tf_op | source)
XLA Modules:
  0.0 183.3 jit_solution(11200617808403689420)
XLA Ops:
  0.7 172.6 %shard_map.254 = (bf16[512,512]{1,0:T(8,128)(2,1)}, f32[512,512]{1,0:T(8,128)}, bf16[1536,512]{1,0:T(8,128)(2,1)}, bf16[512,512]{1,0:T(8,128)(2,1)}, bf16[512,20...) custom-call(bf16[1024,512]{1,0:T(8,128)(2,1)} %hid.1, s32[8,128]{1,0:T(8,128)} %bitcast.26, ...), custom_call_target="tpu_custom_call" | custom-call | tf_op jit(solution)/shard_map/pallas_call | solution.py:787
  173.3 9.8 %shard_map.255 = (bf16[512,512]{1,0:T(8,128)(2,1)}, f32[512,512]{1,0:T(8,128)}, f32[1536,512]{1,0:T(8,128)}, f32[512,512]{1,0:T(8,128)}, f32[512,2048]{1,0:T(8,1...) custom-call(bf16[512,512]{1,0:T(8,128)(2,1)} %get-tuple-element.35.h, ...), custom_call_target="tpu_custom_call" | custom-call | tf_op jit(solution)/shard_map/pallas_call | solution.py:863

commit v5 on v4

--- a/solution.py
+++ b/solution.py
@@ -107,13 +107,14 @@
         self.make(q, step).wait_recv()
         if step > 4:
             return
-        size, chunk = self.size(min(step + 1, 4)), 32
+        size = self.size(min(step + 1, 4))
+        chunk = min(size, 64)
         offset, place = self.offsets[q][min(step + 1, 4)], self.places[q][step]
 
         def add(i, carry):
             here = pl.ds(pl.multiple_of(offset + i * chunk, 16), chunk)
             there = self.landing(q, pl.multiple_of(place + i * chunk, 16), chunk)
-            total = (self.buf[here, :].astype(F32) + there[...].astype(F32)).astype(BF)
+            total = self.buf[here, :] + there[...]
             if step == 4:
                 first = self.fin_base + q * size
                 self.fin[pl.ds(pl.multiple_of(first + i * chunk, 16), chunk), :] = total
@@ -680,14 +681,13 @@
     back_pair(0, 1)
     dqkv_got = [send_qkv(0)]
     passed = [pass_on(grad_attn, c, ga_sent[c][0]) for c in range(CHUNKS)]
-    sum1.advance(1)
     for copy in passed:
         copy.wait_recv()
     context_back(1)
     back_pair(1, 0)
+    sum1.advance(1)
     back_pair(1, 1)
     dqkv_got.append(send_qkv(1))
-    sum1.advance(2)
 
     for part, ctx in enumerate((ctx_own, ctx_o)):
         side = n if part == 0 else 1 - n
@@ -695,6 +695,7 @@
         packed[span(OUT_BASE + side * 256, 256), :] = got.astype(BF)
     for s in range(2):
         column_add(SMALL_OUT, ga_own[s].astype(F32))
+    sum1.advance(2)
     dqkv_got[0].wait_recv()
     dqkv_got[1].wait_recv()
     for part, g in enumerate((act_own, slope)):
@@ -850,7 +851,7 @@
 
 
 def finish_call(hidden, grad, qkv, out, up, down, small):
-    steps = 8
+    steps = 16
 
     def rows(shape):
         return pl.BlockSpec((shape[0] // steps, shape[1]), lambda i: (i, 0))

time: 184 us -> 186 us (1.011)
  Pallas kernels: 182 us -> 184 us
    pallas_call x1, Pallas kernels: 9.82 us -> 13.9 us  [finish_call(): pl.pallas_call(finish_kernel, grid=(steps,), out_shape=[jax.ShapeDtypeStr...]
    pallas_call x1, Pallas kernels: 173 us -> 170 us  [layer_call(): pl.pallas_call(layer_kernel, out_shape=(jax.ShapeDtypeStruct((SEQ, 512),...]
where the time goes in v5:
time: 186 us; the launch traced here: 184 us
  Pallas kernels  184 us (99%)
    pallas_call x1, Pallas kernels, layer_call(): pl.pallas_call(layer_kernel, out_shape=(jax.ShapeDtypeStruct((SEQ, 512),...  170 us
    pallas_call x1, Pallas kernels, finish_call(): pl.pallas_call(finish_kernel, grid=(steps,), out_shape=[jax.ShapeDtypeStr...  13.9 us

profile of v5, /device:TPU:0, one launch (start us, length us, event | category | flops | bytes accessed | tf_op | source)
XLA Modules:
  0.0 184.4 jit_solution(10830430370497974557)
XLA Ops:
  0.7 169.6 %shard_map.254 = (bf16[512,512]{1,0:T(8,128)(2,1)}, f32[512,512]{1,0:T(8,128)}, bf16[1536,512]{1,0:T(8,128)(2,1)}, bf16[512,512]{1,0:T(8,128)(2,1)}, bf16[512,20...) custom-call(bf16[1024,512]{1,0:T(8,128)(2,1)} %hid.1, s32[8,128]{1,0:T(8,128)} %bitcast.26, ...), custom_call_target="tpu_custom_call" | custom-call | tf_op jit(solution)/shard_map/pallas_call | solution.py:788
  170.3 13.9 %shard_map.255 = (bf16[512,512]{1,0:T(8,128)(2,1)}, f32[512,512]{1,0:T(8,128)}, f32[1536,512]{1,0:T(8,128)}, f32[512,512]{1,0:T(8,128)}, f32[512,2048]{1,0:T(8,1...) custom-call(bf16[512,512]{1,0:T(8,128)(2,1)} %get-tuple-element.35.h, ...), custom_call_target="tpu_custom_call" | custom-call | tf_op jit(solution)/shard_map/pallas_call | solution.py:864
